TPU v7x, 32 devices: a whole 2x2x4 slice. The times are simulated.
32 devices in a mesh: row: 16 (over z, y, core), col: 2 (over x).
Axes of the slice: x: 2, y: 2, z: 4, core: 2. Of those that a mesh axis runs over, the one named last changes fastest.
Arguments:
- feature_map: bfloat16 [128, 64, 384], P('row', 'col'), may hold values from -6 to 6
- kernel: float32 [7, 7, 384], replicated, may hold values from -0.875 to 0.875
- ln_gain: float32 [384], replicated, may hold values from 0.5 to 1.5
- ln_bias: float32 [384], replicated, may hold values from -3 to 3
- w_in: bfloat16 [384, 1536], P(None, ('row', 'col')), may hold values from -0.3125 to 0.3125
- b_in: float32 [1536], replicated, may hold values from -3 to 3
- w_out: bfloat16 [1536, 384], P(('row', 'col')), may hold values from -0.15625 to 0.15625
- b_out: float32 [384], replicated, may hold values from -3 to 3
- layer_scale: float32 [384], replicated, may hold values from 0.5 to 1.5
- cotangent: bfloat16 [128, 64, 384], P('row', 'col'), may hold values from -6 to 6
Outputs:
- block_out: bfloat16 [128, 64, 384], P('row', 'col')
- grad_input: bfloat16 [128, 64, 384], P('row', 'col')
- grad_w_in: float32 [384, 1536], P(None, ('row', 'col'))
- grad_w_out: float32 [1536, 384], P(('row', 'col'))
- small_grads: float32 [53, 384], replicated
- grad_b_in: float32 [1536], replicated
All inputs are finite; a program needn't handle non-finite values.
Results may differ from a plain program's by a relative error of at most 0.007.
Values may be sent and summed in bfloat16 or wider, within the bound.
A program may use at most 64 MiB of HBM per device.

v0:
```python
import math

import jax
import jax.numpy as jnp
from jax import lax
from jax.sharding import PartitionSpec as P


def padded_2(x, sides, width):
    for axis, dim in sides:
        peers, length = (lax.axis_size(axis), x.shape[dim])
        up = [(i, (i + 1) % peers) for i in range(peers - 1)]
        down = [(j, i) for i, j in up]
        last = lax.slice_in_dim(x, length - width, length, axis=dim)
        first = lax.slice_in_dim(x, 0, width, axis=dim)
        before = lax.ppermute(last, axis, up)
        after = lax.ppermute(first, axis, down)
        x = jnp.concatenate([before, x, after], axis=dim)
    return x


def gelu_parts(hidden):
    normal_cdf = 0.5 * (1.0 + jax.scipy.special.erf(hidden * (1.0 / math.sqrt(2.0))))
    density = jnp.exp(-0.5 * hidden * hidden) * (1.0 / math.sqrt(2.0 * math.pi))
    return (hidden * normal_cdf, normal_cdf + hidden * density)


def extend(field):
    return padded_2(field, (("row", 0), ("col", 1)), 3)


def on_device(
    feature_map, kernel, ln_gain, ln_bias, w_in, b_in, w_out, b_out, layer_scale, cotangent
):
    row_count, col_count, channels = feature_map.shape
    pixels = row_count * col_count
    padded = extend(feature_map).astype(jnp.float32)
    conv = jnp.zeros((row_count, col_count, channels), jnp.float32)
    for tap_row in range(7):
        for tap_col in range(7):
            conv = (
                conv
                + padded[tap_row : tap_row + row_count, tap_col : tap_col + col_count]
                * kernel[tap_row, tap_col]
            )
    average = jnp.mean(conv, -1, keepdims=True)
    centered = conv - average
    variance = jnp.mean(centered * centered, -1, keepdims=True)
    inv_std = lax.rsqrt(variance + 1e-06)
    unit_scaled = centered * inv_std
    normed = (unit_scaled * ln_gain + ln_bias).astype(jnp.bfloat16).reshape(pixels, channels)
    contract_last = (((1,), (1,)), ((), ()))
    contract_first = (((0,), (0,)), ((), ()))
    w_in_full = lax.all_gather(w_in, ("row", "col"), axis=1, tiled=True)
    w_out_full = lax.all_gather(w_out, ("row", "col"), axis=0, tiled=True)
    hidden = jnp.dot(normed, w_in_full, preferred_element_type=jnp.float32) + b_in
    act_value, slope = gelu_parts(hidden)
    activated = act_value.astype(jnp.bfloat16)
    mixed = jnp.dot(activated, w_out_full, preferred_element_type=jnp.float32) + b_out
    source = feature_map.astype(jnp.float32).reshape(pixels, channels)
    block_out = (
        (source + layer_scale * mixed).astype(jnp.bfloat16).reshape(row_count, col_count, channels)
    )
    grad_flow = cotangent.astype(jnp.float32).reshape(pixels, channels)
    grad_mixed = grad_flow * layer_scale
    mixed_low = grad_mixed.astype(jnp.bfloat16)
    grad_act = lax.dot_general(
        mixed_low, w_out_full, contract_last, preferred_element_type=jnp.float32
    )
    grad_hidden = (grad_act * slope).astype(jnp.bfloat16)
    grad_w_out = lax.psum_scatter(
        lax.dot_general(activated, mixed_low, contract_first, preferred_element_type=jnp.float32),
        ("row", "col"),
        scatter_dimension=0,
        tiled=True,
    )
    win_term = lax.dot_general(
        normed, grad_hidden, contract_first, preferred_element_type=jnp.float32
    )
    grad_w_in = lax.psum_scatter(win_term, ("row", "col"), scatter_dimension=1, tiled=True)
    grad_normed = lax.dot_general(
        grad_hidden, w_in_full, contract_last, preferred_element_type=jnp.float32
    )
    grad_normed = grad_normed.reshape(row_count, col_count, channels)
    grad_gain = jnp.sum(grad_normed * unit_scaled, (0, 1))
    grad_lnb = jnp.sum(grad_normed, (0, 1))
    scaled_grad = grad_normed * ln_gain
    grad_conv = inv_std * (
        scaled_grad
        - jnp.mean(scaled_grad, -1, keepdims=True)
        - unit_scaled * jnp.mean(scaled_grad * unit_scaled, -1, keepdims=True)
    )
    tap_terms = []
    for tap_row in range(7):
        for tap_col in range(7):
            tap_terms.append(
                jnp.sum(
                    padded[tap_row : tap_row + row_count, tap_col : tap_col + col_count]
                    * grad_conv,
                    (0, 1),
                )
            )
    grad_pad = extend(grad_conv.astype(jnp.bfloat16)).astype(jnp.float32)
    back_conv = jnp.zeros((row_count, col_count, channels), jnp.float32)
    for tap_row in range(7):
        for tap_col in range(7):
            back_conv = (
                back_conv
                + grad_pad[
                    6 - tap_row : 6 - tap_row + row_count, 6 - tap_col : 6 - tap_col + col_count
                ]
                * kernel[tap_row, tap_col]
            )
    grad_input = (cotangent.astype(jnp.float32) + back_conv).astype(jnp.bfloat16)
    small_local = jnp.concatenate(
        [
            jnp.stack(tap_terms, 0),
            grad_gain[None],
            grad_lnb[None],
            jnp.sum(grad_mixed, 0)[None],
            jnp.sum(grad_flow * mixed, 0)[None],
        ],
        0,
    )
    bias_local = jnp.sum(grad_hidden.astype(jnp.float32), 0)
    small_grads, grad_b_in = lax.psum((small_local, bias_local), ("row", "col"))
    return (block_out, grad_input, grad_w_in, grad_w_out, small_grads, grad_b_in)


def solution(mesh):
    placed = (
        P("row", "col", None),
        P(),
        P(),
        P(),
        P(None, ("row", "col")),
        P(),
        P(("row", "col"), None),
        P(),
        P(),
        P("row", "col", None),
    )
    return jax.shard_map(
        on_device,
        mesh=mesh,
        in_specs=placed,
        out_specs=(
            P("row", "col", None),
            P("row", "col", None),
            P(None, ("row", "col")),
            P(("row", "col"), None),
            P(),
            P(),
        ),
        check_vma=False,
    )
```

profile of v0, /device:TPU:0, one launch (start us, length us, event | category | flops | bytes accessed | tf_op | source)
XLA Modules:
  0.0 473.8 jit_solution(11672724158360896982)
XLA Ops:
  7.2 0.0 all-gather.3.cloned.1.call-start
  7.2 0.7 all-gather.3.cloned.1.call-update
  7.9 0.0 all-gather.5.cloned.1.call-start
  7.9 0.9 fusion.63
  8.9 2.4 collective-permute-start
  11.3 1.3 collective-permute-start.1
  12.6 0.0 all-gather.5.cloned.1.call-update
  12.6 0.0 all-reduce.2.cloned.1.call-start
  12.6 1.3 slice_reduce_fusion.47
  13.9 1.0 fusion.56
  14.9 1.3 slice_reduce_fusion.48
  16.2 0.0 collective-permute-done
  16.2 1.0 constant_dynamic-update-slice_fusion.1
  17.2 0.0 collective-permute-done.1
  17.2 4.2 collective-permute-start.2
  21.5 1.3 collective-permute-start.3
  22.8 1.0 slice_reduce_fusion.46
  23.7 0.0 collective-permute-done.2
  23.8 3.6 collective-permute-done.3
  27.4 0.1 maximum_convert_fusion
  27.5 0.0 copy-start.6
  27.5 0.0 copy-start.8
  27.5 0.0 copy-start.7
  27.6 3.1 fusion.60
  30.7 0.2 multiply_reduce_fusion.52
  30.9 0.1 add_convert_fusion
  31.1 36.7 %all-gather.3.cloned.1.call-done = bf16[384,1536]{0,1:T(8,128)(2,1)} async-done(((bf16[384,48]{0,1:T(8,128)(2,1)}), bf16[384,1536]{0,1:T(8,128)(2,1)}) %all-gather.3.cloned.1.call-update) | async-done | bytes 1179664 | tf_op jit(solution)/shard_map/all_gather | solution.py:54
  67.8 0.0 copy-done.7
  67.8 0.0 copy-start.11
  67.8 3.1 multiply_convert_fusion
  70.9 52.9 %all-gather.5.cloned.1.call-done = bf16[1536,384]{1,0:T(8,128)(2,1)} async-done(((bf16[48,384]{1,0:T(8,128)(2,1)}), bf16[1536,384]{1,0:T(8,128)(2,1)}) %all-gather.5.cloned.1.call-update) | async-done | bytes 1179664 | tf_op jit(solution)/shard_map/all_gather | solution.py:55
  123.9 2.7 fusion.58
  126.6 0.9 convert_reduce_fusion
  127.5 0.3 copy-done.1
  127.9 0.7 fusion.59
  128.5 0.2 multiply_reduce_fusion
  128.8 0.1 div.17
  128.9 0.9 multiply_reduce_fusion.1
  129.8 0.6 multiply_reduce_fusion.37
  130.3 0.7 multiply_reduce_fusion.19
  131.6 4.4 concatenate.19
  136.0 0.0 all-reduce.2.cloned.1.call-update
  136.0 0.0 reduce-scatter.5.cloned.1.call-start
  136.1 2.0 fusion.65
  138.1 0.0 reduce-scatter.5.cloned.1.call-update
  138.1 0.0 reduce-scatter.3.cloned.1.call-start
  138.2 1.1 copy-done.4
  139.2 2.0 fusion.64
  141.2 0.0 reduce-scatter.3.cloned.1.call-update
  141.3 2.2 collective-permute-start.4
  143.5 1.3 collective-permute-start.5
  144.8 0.0 collective-permute-done.4
  144.8 2.7 collective-permute-done.5
  147.5 2.5 collective-permute-start.6
  150.0 1.3 collective-permute-start.7
  151.3 42.7 %psum.15 = f32[1536]{0:T(1024)} all-reduce(f32[1536]{0:T(1024)S(1)} %get-tuple-element.126), channel_id=1, replica_groups=mesh['row'=16,'col'=2] {'row','col'}, use_global_device_ids=true, to_apply=%region_61.0 | all-reduce | flops 1536 | bytes 12288 | tf_op jit(solution)/shard_map/psum | solution.py:126
  194.0 0.0 collective-permute-done.6
  194.0 0.0 collective-permute-done.7
  194.0 0.1 maximum_convert_fusion.1
  194.2 3.5 fusion.7
  197.7 56.9 %all-reduce.2.cloned.1.call-done = f32[53,384]{1,0:T(8,128)} async-done(((f32[53,384]{1,0:T(8,128)}), f32[53,384]{1,0:T(8,128)}) %all-reduce.2.cloned.1.call-update) | async-done | bytes 81424 | tf_op jit(solution)/shard_map/psum | solution.py:126
  254.6 106.6 %reduce-scatter.5.cloned.1.call-done = f32[48,384]{1,0:T(8,128)} async-done(((f32[1536,384]{1,0:T(8,128)}), f32[48,384]{1,0:T(8,128)}) %reduce-scatter.5.cloned.1.call-update) | async-done | bytes 73744 | tf_op jit(solution)/shard_map/reduce_scatter | solution.py:71
  361.2 104.6 %reduce-scatter.3.cloned.1.call-done = f32[384,48]{0,1:T(8,128)} async-done(((f32[384,1536]{0,1:T(8,128)}), f32[384,48]{0,1:T(8,128)}) %reduce-scatter.3.cloned.1.call-update) | async-done | bytes 73744 | tf_op jit(solution)/shard_map/reduce_scatter | solution.py:80
  465.8 1.5 copy.19
  (79 shorter events, 0.3 us)
Async XLA Ops:
  7.2 60.6 %all-gather.3.cloned.1.call-start = ((), (), s32[]{:S(2)}) async-start(), calls=%async_computation.2 | async-start | bytes 1216512 | tf_op jit(solution)/shard_map/all_gather | solution.py:54
  7.9 115.9 %all-gather.5.cloned.1.call-start = ((), (), s32[]{:S(2)}) async-start(), calls=%async_computation.3 | async-start | bytes 1216512 | tf_op jit(solution)/shard_map/all_gather | solution.py:55
  8.9 7.3 %collective-permute-start = (bf16[3,32,384]{2,1,0:T(8,128)(2,1)S(1)}, bf16[3,32,384]{2,1,0:T(8,128)(2,1)S(1)}, u32[]{:S(2)}, u32[]{:S(2)}) collective-permute-start(bf16[3,32,384]{2,1,0:T(8,128)(2,1)S(1)} %get-tuple-element.122), channel_id=1, source_target_pairs={{0,2},{2,4},{4,6},{6,8},{8,10},{10,12},{12,14},{14,16},{16,18},{18... | collective-permute-start | bytes 221192 | tf_op jit(solution)/shard_map/ppermute | solution.py:16
  11.3 5.9 %collective-permute-start.1 = (bf16[3,32,384]{2,1,0:T(8,128)(2,1)S(1)}, bf16[3,32,384]{2,1,0:T(8,128)(2,1)S(1)}, u32[]{:S(2)}, u32[]{:S(2)}) collective-permute-start(bf16[3,32,384]{2,1,0:T(8,128)(2,1)S(1)} %get-tuple-element.121), channel_id=1, source_target_pairs={{2,0},{4,2},{6,4},{8,6},{10,8},{12,10},{14,12},{16,14},{18,16},{20... | collective-permute-start | bytes 221192 | tf_op jit(solution)/shard_map/ppermute | solution.py:17
  12.6 242.0 %all-reduce.2.cloned.1.call-start = ((), (), s32[]{:S(2)}) async-start(), calls=%async_computation.6 | async-start | bytes 172032 | tf_op jit(solution)/shard_map/psum | solution.py:126
  17.2 6.5 %collective-permute-start.2 = (bf16[14,3,384]{2,1,0:T(4,128)(2,1)S(1)}, bf16[14,3,384]{2,1,0:T(4,128)(2,1)S(1)}, u32[]{:S(2)}, u32[]{:S(2)}) collective-permute-start(bf16[14,3,384]{2,1,0:T(4,128)(2,1)S(1)} %get-tuple-element.116), channel_id=1, source_target_pairs={{0,1},{2,3},{4,5},{6,7},{8,9},{10,11},{12,13},{14,15},{16,17},{18,... | collective-permute-start | bytes 96776 | tf_op jit(solution)/shard_map/ppermute | solution.py:16
  21.5 5.9 %collective-permute-start.3 = (bf16[14,3,384]{2,1,0:T(4,128)(2,1)S(1)}, bf16[14,3,384]{2,1,0:T(4,128)(2,1)S(1)}, u32[]{:S(2)}, u32[]{:S(2)}) collective-permute-start(bf16[14,3,384]{2,1,0:T(4,128)(2,1)S(1)} %get-tuple-element.117), channel_id=1, source_target_pairs={{1,0},{3,2},{5,4},{7,6},{9,8},{11,10},{13,12},{15,14},{17,16},{19,... | collective-permute-start | bytes 96776 | tf_op jit(solution)/shard_map/ppermute | solution.py:17
  27.5 3.4 copy-start.6
  27.5 3.4 copy-start.8
  27.5 40.3 %copy-start.7 = (f32[1536]{0:T(1024)S(1)}, f32[1536]{0:T(1024)}, u32[]{:S(2)}) copy-start(f32[1536]{0:T(1024)} %param.15) | copy-start | bytes 18436
  67.8 56.0 %copy-start.2 = (bf16[8,32,384]{2,1,0:T(8,128)(2,1)S(1)}, bf16[8,32,384]{2,1,0:T(8,128)(2,1)}, u32[]{:S(2)}) copy-start(bf16[8,32,384]{2,1,0:T(8,128)(2,1)} %param.19) | copy-start | bytes 589828
  67.8 56.0 %copy-start.5 = (bf16[8,32,384]{2,1,0:T(8,128)(2,1)S(1)}, bf16[8,32,384]{2,1,0:T(8,128)(2,1)}, u32[]{:S(2)}) copy-start(bf16[8,32,384]{2,1,0:T(8,128)(2,1)} %param.10) | copy-start | bytes 589828
  67.8 56.0 %copy-start.9 = (f32[384]{0:T(512)S(1)}, f32[384]{0:T(512)}, u32[]{:S(2)}) copy-start(f32[384]{0:T(512)} %param.18) | copy-start | bytes 4612
  67.8 56.0 %copy-start.11 = (f32[384]{0:T(512)S(1)}, f32[384]{0:T(512)}, u32[]{:S(2)}) copy-start(f32[384]{0:T(512)} %param.17) | copy-start | bytes 4612
  123.8 2.8 copy-start
  123.8 2.8 copy-start.10
  126.6 1.3 copy-start.1
  127.5 1.2 copy-start.3
  136.0 225.1 %reduce-scatter.5.cloned.1.call-start = ((), (), s32[]{:S(2)}) async-start(), calls=%async_computation.5 | async-start | bytes 2433024 | tf_op jit(solution)/shard_map/reduce_scatter | solution.py:71
  138.1 1.1 copy-start.4
  138.1 327.7 %reduce-scatter.3.cloned.1.call-start = ((), (), s32[]{:S(2)}) async-start(), calls=%async_computation.4 | async-start | bytes 2433024 | tf_op jit(solution)/shard_map/reduce_scatter | solution.py:80
  141.3 3.5 collective-permute-start.4
  143.5 4.0 collective-permute-start.5
  147.5 46.5 %collective-permute-start.6 = (bf16[14,3,384]{2,1,0:T(4,128)(2,1)S(1)}, bf16[14,3,384]{2,1,0:T(4,128)(2,1)S(1)}, u32[]{:S(2)}, u32[]{:S(2)}) collective-permute-start(bf16[14,3,384]{2,1,0:T(4,128)(2,1)S(1)} %get-tuple-element.114), channel_id=1, source_target_pairs={{0,1},{2,3},{4,5},{6,7},{8,9},{10,11},{12,13},{14,15},{16,17},{18,... | collective-permute-start | bytes 96776 | tf_op jit(solution)/shard_map/ppermute | solution.py:16
  150.0 44.0 %collective-permute-start.7 = (bf16[14,3,384]{2,1,0:T(4,128)(2,1)S(1)}, bf16[14,3,384]{2,1,0:T(4,128)(2,1)S(1)}, u32[]{:S(2)}, u32[]{:S(2)}) collective-permute-start(bf16[14,3,384]{2,1,0:T(4,128)(2,1)S(1)} %get-tuple-element.115), channel_id=1, source_target_pairs={{1,0},{3,2},{5,4},{7,6},{9,8},{11,10},{13,12},{15,14},{17,16},{19,... | collective-permute-start | bytes 96776 | tf_op jit(solution)/shard_map/ppermute | solution.py:17
Sparse Core Ops, SparseCore 0:
  10.9 56.8 all-gather.2
  70.7 53.0 all-gather.4
  136.1 118.3 all-reduce.1
  260.3 100.8 reduce-scatter.4
  367.7 97.9 reduce-scatter.2
where the time goes:
time: 475 us; the launch traced here: 474 us
  waiting for transfers between devices  365 us (77%)
  blocking collectives  42.7 us (9%)
  starting transfers between devices  16.7 us (4%)
  between operations  14.5 us (3%)
  local copies, waits for them, and re-layouts  13 us (3%)
  matrix products  11.4 us (2%)
  other arithmetic  10.7 us (2%)
    reduce_scatter x1, waiting for transfers between devices, on_device(): lax.psum_scatter(lax.dot_general(activated, mixed_low, contract_first, pr...  107 us
    reduce_scatter x1, waiting for transfers between devices, on_device(): lax.psum_scatter(win_term, ('row', 'col'), scatter_dimension=1, tiled=True)  105 us
    psum x1, waiting for transfers between devices, on_device(): small_grads, grad_b_in = lax.psum((small_local, bias_local), ('row', 'col'))  56.9 us
    all_gather x1, waiting for transfers between devices, on_device(): w_out_full = lax.all_gather(w_out, ('row', 'col'), axis=0, tiled=True)  52.9 us
    psum x1, blocking collectives, on_device(): small_grads, grad_b_in = lax.psum((small_local, bias_local), ('row', 'col'))  42.7 us
    all_gather x1, waiting for transfers between devices, on_device(): w_in_full = lax.all_gather(w_in, ('row', 'col'), axis=1, tiled=True)  36.7 us
    ppermute x4, starting transfers between devices, padded_2(): before = lax.ppermute(last, axis, up)  11.3 us
  transfers between devices with their start and end apart: 13, of which 7 were waited for; matrix products, arithmetic and copies ran while one was open for 4% of the time, Pallas kernels for 0%

commit v1 on v0

--- a/solution.py
+++ b/solution.py
@@ -1,8 +1,11 @@
+import functools
 import math
 
 import jax
 import jax.numpy as jnp
 from jax import lax
+from jax.experimental import pallas as pl
+from jax.experimental.pallas import tpu as pltpu
 from jax.sharding import PartitionSpec as P
 
 
@@ -29,7 +32,7 @@
     return padded_2(field, (("row", 0), ("col", 1)), 3)
 
 
-def on_device(
+def spread_plan(
     feature_map, kernel, ln_gain, ln_bias, w_in, b_in, w_out, b_out, layer_scale, cotangent
 ):
     row_count, col_count, channels = feature_map.shape
@@ -127,6 +130,443 @@
     return (block_out, grad_input, grad_w_in, grad_w_out, small_grads, grad_b_in)
 
 
+MESH = pl.DeviceIdType.MESH
+SIDES = [(a, b) for a in (-1, 0, 1) for b in (-1, 0, 1) if (a, b) != (0, 0)]
+EDGE = 16
+LANES = 128
+CONTRACT_LAST = (((1,), (1,)), ((), ()))
+CONTRACT_FIRST = (((0,), (0,)), ((), ()))
+
+
+def bit_orders(rows, cols):
+    bits = (rows * cols).bit_length() - 1
+    pair = cols.bit_length() - 1
+    rest = [b for b in range(bits - 1, -1, -1) if b != pair]
+    orders = [rest, rest[-1:] + rest[:-1], rest[-2:] + rest[:-2]]
+    return [order + [pair] for order in orders]
+
+
+def fused_kernel(
+    rows,
+    cols,
+    orders,
+    x_ref,
+    taps_ref,
+    vec_ref,
+    bin_ref,
+    shard_ref,
+    cot_ref,
+    out_ref,
+    gin_ref,
+    gwin_ref,
+    gwout_ref,
+    small_ref,
+    gbin_ref,
+    xpad,
+    gpad,
+    wide,
+    conv,
+    unit,
+    normed,
+    mixed_low,
+    mixed,
+    gnorm,
+    weights,
+    total,
+    leaving,
+    arriving,
+    sums,
+    sums_in,
+    halo_send,
+    halo_recv,
+    gather_send,
+    gather_recv,
+    scatter_send,
+    scatter_recv,
+    sum_send,
+    sum_recv,
+):
+    height, width, channels = x_ref.shape
+    pixels = height * width
+    parts = len(orders)
+    steps = len(orders[0])
+    unit_rows = shard_ref.shape[2]
+    chunk = weights.shape[2] * unit_rows
+    row, col = lax.axis_index("row"), lax.axis_index("col")
+    me = row * cols + col
+    f32, bf16 = jnp.float32, jnp.bfloat16
+
+    def bit_of(b):
+        return lax.rem(lax.div(me, 2**b), 2)
+
+    def partner(b):
+        other = me + (1 - 2 * bit_of(b)) * 2**b
+        return (lax.div(other, cols), lax.rem(other, cols))
+
+    places = []
+    for order in orders:
+        place = 0
+        for step, b in enumerate(order):
+            place = place + bit_of(b) * 2**step
+        places.append(place)
+
+    def exists(side):
+        dr, dc = side
+        there = None
+        for delta, at, count in ((dr, row, rows), (dc, col, cols)):
+            if delta:
+                ok = at > 0 if delta < 0 else at < count - 1
+                there = ok if there is None else jnp.logical_and(there, ok)
+        return there
+
+    def halo_copy(source, pad, which, side, receiving):
+        dr, dc = side
+        at = SIDES.index(side)
+        back = SIDES.index((-dr, -dc))
+        row_from = {-1: pl.ds(0, 3), 0: pl.ds(0, height), 1: pl.ds(height - 3, 3)}[dr]
+        col_from = {-1: pl.ds(0, EDGE), 0: pl.ds(0, width), 1: pl.ds(width - EDGE, EDGE)}[dc]
+        into_r, into_c = (dr, dc) if receiving else (-dr, -dc)
+        row_to = {-1: pl.ds(0, 3), 0: pl.ds(3, height), 1: pl.ds(height + 3, 3)}[into_r]
+        col_to = {-1: pl.ds(0, EDGE), 0: pl.ds(EDGE, width), 1: pl.ds(width + EDGE, EDGE)}[into_c]
+        return pltpu.make_async_remote_copy(
+            src_ref=source.at[row_from, col_from],
+            dst_ref=pad.at[row_to, col_to],
+            send_sem=halo_send.at[which, at],
+            recv_sem=halo_recv.at[which, back if receiving else at],
+            device_id=(row + dr, col + dc),
+            device_id_type=MESH,
+        )
+
+    def halo_start(source, pad, which):
+        for side in SIDES:
+
+            @pl.when(exists(side))
+            def _():
+                halo_copy(source, pad, which, side, False).start()
+
+    def halo_wait(source, pad, which):
+        for side in SIDES:
+
+            @pl.when(exists(side))
+            def _():
+                halo_copy(source, pad, which, side, False).wait_send()
+                halo_copy(source, pad, which, side, True).wait_recv()
+
+    def gather_copy(part, step):
+        size = 2**step
+        held = weights.at[part, :, pl.ds(lax.div(places[part], size) * size, size)]
+        return pltpu.make_async_remote_copy(
+            src_ref=held,
+            dst_ref=held,
+            send_sem=gather_send.at[part, step],
+            recv_sem=gather_recv.at[part, step],
+            device_id=partner(orders[part][step]),
+            device_id_type=MESH,
+        )
+
+    def gather_turn(part, step):
+        if step:
+            gather_copy(part, step - 1).wait()
+        if step < steps:
+            gather_copy(part, step).start()
+
+    def scatter_copy(part, step):
+        size = 2**step
+        return pltpu.make_async_remote_copy(
+            src_ref=leaving.at[part, :, pl.ds(size, size)],
+            dst_ref=arriving.at[part, :, pl.ds(size, size)],
+            send_sem=scatter_send.at[part, step],
+            recv_sem=scatter_recv.at[part, step],
+            device_id=partner(orders[part][step]),
+            device_id_type=MESH,
+        )
+
+    def scatter_start(part, step):
+        size = 2**step
+        mine = lax.div(places[part], size)
+        away = (mine + 1 - 2 * lax.rem(mine, 2)) * size
+        leaving[part, :, size : 2 * size] = total[part, :, pl.ds(away, size)].astype(bf16)
+        scatter_copy(part, step).start()
+
+    def scatter_turn(part, step):
+        size = 2**step
+        scatter_copy(part, step).wait()
+        keep = pl.ds(lax.div(places[part], size) * size, size)
+        total[part, :, keep] = total[part, :, keep] + arriving[part, :, size : 2 * size].astype(f32)
+        if step:
+            scatter_start(part, step - 1)
+
+    def scatter_turns(step):
+        for part in range(parts):
+            scatter_turn(part, step)
+
+    def sum_copy(step):
+        return pltpu.make_async_remote_copy(
+            src_ref=sums.at[step],
+            dst_ref=sums_in.at[step],
+            send_sem=sum_send.at[step],
+            recv_sem=sum_recv.at[step],
+            device_id=partner(orders[0][steps - 1 - step]),
+            device_id_type=MESH,
+        )
+
+    def sum_turn(step):
+        sum_copy(step).wait()
+        sums[step + 1] = sums[step] + sums_in[step]
+        if step + 1 < steps:
+            sum_copy(step + 1).start()
+
+    gain, offset = vec_ref[0:1, :], vec_ref[1:2, :]
+    out_bias, scale = vec_ref[2:3, :], vec_ref[3:4, :]
+
+    xpad[...] = jnp.zeros_like(xpad)
+    gpad[...] = jnp.zeros_like(gpad)
+    for part in range(parts):
+        weights[part, :, pl.ds(places[part], 1)] = shard_ref[part][:, None]
+
+    barrier = pltpu.get_barrier_semaphore()
+    expected = steps
+    for b in range(steps):
+        pl.semaphore_signal(barrier, inc=1, device_id=partner(b), device_id_type=MESH)
+    for side in SIDES:
+        here = exists(side)
+        expected = expected + jnp.where(here, 1, 0)
+
+        @pl.when(here)
+        def _():
+            pl.semaphore_signal(
+                barrier, inc=1, device_id=(row + side[0], col + side[1]), device_id_type=MESH
+            )
+
+    pl.semaphore_wait(barrier, expected)
+
+    halo_start(x_ref, xpad, 0)
+    for part in range(parts):
+        gather_turn(part, 0)
+
+    xpad[3 : 3 + height, EDGE : EDGE + width] = x_ref[...]
+    sums[0, 48:64] = jnp.zeros((16, channels), f32)
+    grad_mixed = cot_ref[...].astype(f32).reshape(pixels, channels) * scale
+    mixed_low[...] = grad_mixed.astype(bf16)
+    sums[0, 51:52] = jnp.sum(grad_mixed, 0, keepdims=True)
+
+    halo_wait(x_ref, xpad, 0)
+    for part in range(parts):
+        gather_turn(part, 1)
+    wide[...] = xpad[:, 8 : width + 24].astype(f32)
+
+    def window(shift, lanes):
+        return wide[:, 5 + shift : 5 + shift + width, lanes]
+
+    def stencil(lanes, flip):
+        result = jnp.zeros((height, width, LANES), f32)
+        for tap_col in range(7):
+            shifted = window(tap_col, lanes)
+            for tap_row in range(7):
+                at = tap_row * 7 + tap_col
+                at = 48 - at if flip else at
+                result = result + shifted[tap_row : tap_row + height] * taps_ref[at : at + 1, lanes]
+        return result
+
+    blocks = channels // LANES
+    for block in range(blocks):
+        lanes = slice(block * LANES, (block + 1) * LANES)
+        conv[:, lanes] = stencil(lanes, False).reshape(pixels, LANES)
+        if block + 2 < steps:
+            for part in range(parts):
+                gather_turn(part, block + 2)
+
+    centered = conv[...]
+    centered = centered - jnp.mean(centered, -1, keepdims=True)
+    inv_std = lax.rsqrt(jnp.mean(centered * centered, -1, keepdims=True) + 1e-06)
+    unit[...] = centered * inv_std
+    normed[...] = (unit[...] * gain + offset).astype(bf16)
+    for step in range(blocks + 2, steps + 1):
+        for part in range(parts):
+            gather_turn(part, step)
+
+    for part in range(parts):
+        win = weights[part, 0].reshape(chunk, channels)
+        wout = weights[part, 1].reshape(chunk, channels)
+        hidden = (
+            lax.dot_general(normed[...], win, CONTRACT_LAST, preferred_element_type=f32)
+            + bin_ref[part : part + 1, :]
+        )
+        act_value, slope = gelu_parts(hidden)
+        activated = act_value.astype(bf16)
+        grad_act = lax.dot_general(
+            mixed_low[...], wout, CONTRACT_LAST, preferred_element_type=f32
+        )
+        grad_hidden = (grad_act * slope).astype(bf16)
+        total[part, 1] = lax.dot_general(
+            activated, mixed_low[...], CONTRACT_FIRST, preferred_element_type=f32
+        ).reshape(-1, unit_rows, channels)
+        total[part, 0] = lax.dot_general(
+            grad_hidden, normed[...], CONTRACT_FIRST, preferred_element_type=f32
+        ).reshape(-1, unit_rows, channels)
+        scatter_start(part, steps - 1)
+        mixed_term = jnp.dot(activated, wout, preferred_element_type=f32)
+        gnorm_term = jnp.dot(grad_hidden, win, preferred_element_type=f32)
+        mixed[...] = mixed_term if part == 0 else mixed[...] + mixed_term
+        gnorm[...] = gnorm_term if part == 0 else gnorm[...] + gnorm_term
+        bias_sum = jnp.sum(grad_hidden.astype(f32), 0, keepdims=True)
+        for piece in range(chunk // LANES):
+            at = part * (chunk // LANES) + piece
+            sums[0, 53 + at // blocks : 54 + at // blocks, at % blocks * LANES : (at % blocks + 1) * LANES] = (
+                bias_sum[:, piece * LANES : (piece + 1) * LANES]
+            )
+
+    scatter_turns(steps - 1)
+    grad_normed = gnorm[...]
+    unit_scaled = unit[...]
+    sums[0, 49:50] = jnp.sum(grad_normed * unit_scaled, 0, keepdims=True)
+    sums[0, 50:51] = jnp.sum(grad_normed, 0, keepdims=True)
+    scaled = grad_normed * gain
+    grad_conv = inv_std * (
+        scaled
+        - jnp.mean(scaled, -1, keepdims=True)
+        - unit_scaled * jnp.mean(scaled * unit_scaled, -1, keepdims=True)
+    )
+    conv[...] = grad_conv
+    normed[...] = grad_conv.astype(bf16)
+    gpad[3 : 3 + height, EDGE : EDGE + width] = normed[...].reshape(height, width, channels)
+    grad_block = gpad.at[pl.ds(3, height), pl.ds(EDGE, width)]
+    halo_start(grad_block, gpad, 1)
+
+    mixed_full = mixed[...] + out_bias
+    source = x_ref[...].astype(f32).reshape(pixels, channels)
+    out_ref[...] = (source + scale * mixed_full).astype(bf16).reshape(height, width, channels)
+    grad_flow = cot_ref[...].astype(f32).reshape(pixels, channels)
+    sums[0, 52:53] = jnp.sum(grad_flow * mixed_full, 0, keepdims=True)
+
+    for block in range(blocks):
+        lanes = slice(block * LANES, (block + 1) * LANES)
+        grad_part = conv[:, lanes].reshape(height, width, LANES)
+        for tap_col in range(7):
+            shifted = window(tap_col, lanes)
+            for tap_row in range(7):
+                at = tap_row * 7 + tap_col
+                term = shifted[tap_row : tap_row + height] * grad_part
+                sums[0, at : at + 1, lanes] = jnp.sum(
+                    term.reshape(pixels, LANES), 0, keepdims=True
+                )
+        if block == 0:
+            scatter_turns(steps - 2)
+    sum_copy(0).start()
+    scatter_turns(steps - 3)
+
+    halo_wait(grad_block, gpad, 1)
+    wide[...] = gpad[:, 8 : width + 24].astype(f32)
+    for block in range(blocks):
+        lanes = slice(block * LANES, (block + 1) * LANES)
+        gin_ref[:, :, lanes] = (
+            cot_ref[:, :, lanes].astype(f32) + stencil(lanes, True)
+        ).astype(bf16)
+        sum_turn(block)
+        if steps - 4 - block >= 0:
+            scatter_turns(steps - 4 - block)
+    for step in range(steps - 4 - blocks, -1, -1):
+        scatter_turns(step)
+    for step in range(blocks, steps):
+        sum_turn(step)
+    for part in range(parts):
+        at = slice(part * unit_rows, (part + 1) * unit_rows)
+        own = total[part, :, pl.ds(places[part], 1)]
+        gwin_ref[at, :] = own[0, 0]
+        gwout_ref[at, :] = own[1, 0]
+    small_ref[...] = sums[steps, 0:53]
+    gbin_ref[...] = sums[steps, 53:57]
+
+
+def on_device(
+    rows,
+    cols,
+    feature_map,
+    kernel,
+    ln_gain,
+    ln_bias,
+    w_in,
+    b_in,
+    w_out,
+    b_out,
+    layer_scale,
+    cotangent,
+):
+    devices = rows * cols
+    parts = 3
+    height, width, channels = feature_map.shape
+    units = w_out.shape[0]
+    steps = devices.bit_length() - 1
+    if units % (16 * parts) or devices != 2**steps or steps < 5 or devices * units != 4 * channels:
+        return spread_plan(
+            feature_map, kernel, ln_gain, ln_bias, w_in, b_in, w_out, b_out, layer_scale, cotangent
+        )
+    orders = bit_orders(rows, cols)
+    piece = units // parts
+    pixels = height * width
+    shard = jnp.stack([w_in.T, w_out]).reshape(2, parts, piece, channels).transpose(1, 0, 2, 3)
+    vectors = jnp.stack([ln_gain, ln_bias, b_out, layer_scale])
+    spread = b_in.reshape((2,) * steps + (parts, piece))
+    bias = jnp.stack(
+        [
+            spread[..., part, :].transpose([steps - 1 - b for b in order[::-1]] + [steps]).reshape(-1)
+            for part, order in enumerate(orders)
+        ]
+    )
+    f32, bf16 = jnp.float32, jnp.bfloat16
+    padded_shape = (height + 6, width + 2 * EDGE, channels)
+    outs = pl.pallas_call(
+        functools.partial(fused_kernel, rows, cols, orders),
+        out_shape=(
+            jax.ShapeDtypeStruct(feature_map.shape, bf16),
+            jax.ShapeDtypeStruct(feature_map.shape, bf16),
+            jax.ShapeDtypeStruct((units, channels), f32),
+            jax.ShapeDtypeStruct((units, channels), f32),
+            jax.ShapeDtypeStruct((53, channels), f32),
+            jax.ShapeDtypeStruct((4, channels), f32),
+        ),
+        in_specs=[pl.BlockSpec(memory_space=pltpu.VMEM)] * 6,
+        out_specs=(pl.BlockSpec(memory_space=pltpu.VMEM),) * 6,
+        scratch_shapes=[
+            pltpu.VMEM(padded_shape, bf16),
+            pltpu.VMEM(padded_shape, bf16),
+            pltpu.VMEM((height + 6, width + 16, channels), f32),
+            pltpu.VMEM((pixels, channels), f32),
+            pltpu.VMEM((pixels, channels), f32),
+            pltpu.VMEM((pixels, channels), bf16),
+            pltpu.VMEM((pixels, channels), bf16),
+            pltpu.VMEM((pixels, channels), f32),
+            pltpu.VMEM((pixels, channels), f32),
+            pltpu.VMEM((parts, 2, devices, piece, channels), bf16),
+            pltpu.VMEM((parts, 2, devices, piece, channels), f32),
+            pltpu.VMEM((parts, 2, devices, piece, channels), bf16),
+            pltpu.VMEM((parts, 2, devices, piece, channels), bf16),
+            pltpu.VMEM((steps + 1, 64, channels), f32),
+            pltpu.VMEM((steps, 64, channels), f32),
+            pltpu.SemaphoreType.DMA((2, len(SIDES))),
+            pltpu.SemaphoreType.DMA((2, len(SIDES))),
+            pltpu.SemaphoreType.DMA((parts, steps)),
+            pltpu.SemaphoreType.DMA((parts, steps)),
+            pltpu.SemaphoreType.DMA((parts, steps)),
+            pltpu.SemaphoreType.DMA((parts, steps)),
+            pltpu.SemaphoreType.DMA((steps,)),
+            pltpu.SemaphoreType.DMA((steps,)),
+        ],
+        compiler_params=pltpu.CompilerParams(
+            collective_id=0, has_side_effects=True, vmem_limit_bytes=50 * 2**20
+        ),
+        name="convnext_block",
+    )(feature_map, kernel.reshape(49, channels), vectors, bias, shard, cotangent)
+    block_out, grad_input, grad_win, grad_wout, small_grads, bias_sums = outs
+    pieces = bias_sums.reshape((parts,) + (2,) * steps + (piece,))
+    ordered = []
+    for part, order in enumerate(orders):
+        back = [steps - 1 - order.index(b) for b in range(steps - 1, -1, -1)]
+        ordered.append(pieces[part].transpose(back + [steps]).reshape(devices, piece))
+    grad_b_in = jnp.stack(ordered, 1).reshape(-1)
+    return (block_out, grad_input, grad_win.T, grad_wout, small_grads, grad_b_in)
+
+
 def solution(mesh):
     placed = (
         P("row", "col", None),
@@ -141,7 +581,7 @@
         P("row", "col", None),
     )
     return jax.shard_map(
-        on_device,
+        functools.partial(on_device, mesh.shape["row"], mesh.shape["col"]),
         mesh=mesh,
         in_specs=placed,
         out_specs=(

time: 475 us -> 75.5 us (0.16)
  waiting for transfers between devices: 365 us -> 0 us
  Pallas kernels: 0 us -> 65.6 us
  blocking collectives: 42.7 us -> 0 us
  starting transfers between devices: 16.7 us -> 0 us
  between operations: 14.5 us -> 0.81 us
  matrix products: 11.4 us -> 0 us
  other arithmetic: 10.7 us -> 0.05 us
    reduce_scatter x2 -> x0, waiting for transfers between devices: 211 us -> none  [the longest x1 107 us: on_device(): lax.psum_scatter(lax.dot_general(activated, mixed_low, contract_first, pr...]
    all_gather x2 -> x0, waiting for transfers between devices: 89.6 us -> none  [the longest x1 52.9 us: on_device(): w_out_full = lax.all_gather(w_out, ('row', 'col'), axis=0, tiled=True)]
    pallas_call x0 -> x1, Pallas kernels: none -> 65.6 us  [on_device(): pl.pallas_call(functools.partial(fused_kernel, rows, cols, orders), out_s...]
    psum x1 -> x0, waiting for transfers between devices: 56.9 us -> none  [on_device(): small_grads, grad_b_in = lax.psum((small_local, bias_local), ('row', 'col'))]
    psum x1 -> x0, blocking collectives: 42.7 us -> none  [on_device(): small_grads, grad_b_in = lax.psum((small_local, bias_local), ('row', 'col'))]
    ppermute x8 -> x0, starting transfers between devices: 16.5 us -> none  [the longest x4 11.3 us: padded_2(): before = lax.ppermute(last, axis, up)]
    dot_general x6 -> x0, matrix products: 11.4 us -> none  [the longest x1 3.12 us: on_device(): jnp.dot(normed, w_in_full, preferred_element_type=jnp.float32) + b_in]
    reduce_sum x7 -> x0, other arithmetic: 6.75 us -> none  [the longest x1 3.14 us: on_device(): average = jnp.mean(conv, -1, keepdims=True)]
  transfers between devices with their start and end apart: 13 -> 0, of which waited for: 7 -> 0; matrix products, arithmetic and copies ran while one was open for 4% -> 0% of each run, Pallas kernels for 0% -> 0%
where the time goes in v1:
time: 75.5 us; the launch traced here: 75.2 us
  Pallas kernels  65.6 us (87%)
  local copies, waits for them, and re-layouts  8.81 us (12%)
  between operations  0.81 us (1%)
    pallas_call x1, Pallas kernels, on_device(): pl.pallas_call(functools.partial(fused_kernel, rows, cols, orders), out_s...  65.6 us
    unnamed x26, local copies, waits for them, and re-layouts  6.6 us

profile of v1, /device:TPU:0, one launch (start us, length us, event | category | flops | bytes accessed | tf_op | source)
XLA Modules:
  0.0 75.2 jit_solution(5651785524602784007)
XLA Ops:
  0.6 0.0 copy-start.5
  0.6 0.9 %reshape.29.taps_ref = f32[49,384]{1,0:T(8,128)S(1)} reshape(f32[7,7,384]{2,1,0:T(8,128)} %param.11) | data formatting | bytes 150528 | tf_op jit(solution)/shard_map/reshape | solution.py:559
  1.6 0.0 copy-done.5
  1.6 0.0 copy-start.6
  1.6 0.7 copy-done.6
  2.2 0.0 copy-start.7
  2.3 0.7 copy-done.7
  2.9 0.0 copy-start.8
  2.9 0.7 copy-done.8
  3.6 0.0 copy-start.4
  3.6 0.7 copy-done.4
  4.3 0.0 copy-start.2
  4.3 0.0 copy-start.3
  4.3 0.1 reshape.30
  4.4 0.0 copy-start
  4.4 0.0 copy-start.1
  4.5 0.1 stack_reshape.20
  4.6 0.1 stack_reshape.19
  4.7 0.1 stack_reshape.18
  4.8 0.2 copy-done.2
  5.1 0.0 copy-done.3
  5.1 0.2 copy-done
  5.4 0.1 copy-done.1
  5.4 65.6 %convnext_block.1 = (bf16[8,32,384]{2,1,0:T(8,128)(2,1)S(1)}, bf16[8,32,384]{2,1,0:T(8,128)(2,1)S(1)}, f32[48,384]{1,0:T(8,128)S(1)}, f32[48,384]{1,0:T(8,128)S(...) custom-call(bf16[8,32,384]{2,1,0:T(8,128)(2,1)S(1)} %copy-done, f32[49,384]{1,0:T(8,128)S(1)} %reshape.29.taps_ref, ...), custom_call_target="tpu_custom_call" | custom-call | tf_op jit(solution)/shard_map/convnext_block/pallas_call | solution.py:518
  71.0 0.1 reshape.31
  71.3 0.7 reshape.32
  72.0 0.7 copy.33
  72.7 0.7 copy.34
  73.3 0.6 copy.35
  74.0 0.6 copy.36
  74.6 0.6 copy.37
  (17 shorter events, 0.2 us)
Async XLA Ops:
  0.6 0.9 %copy-start.5 = (f32[384]{0:T(512)S(1)}, f32[384]{0:T(512)}, u32[]{:S(2)}) copy-start(f32[384]{0:T(512)} %param.18) | copy-start | bytes 4612
  1.6 0.7 copy-start.6
  2.2 0.7 copy-start.7
  2.9 0.7 copy-start.8
  3.6 0.7 copy-start.4
  4.3 0.8 %copy-start.2 = (bf16[48,384]{1,0:T(8,128)(2,1)S(1)}, bf16[48,384]{1,0:T(8,128)(2,1)}, u32[]{:S(2)}) copy-start(bf16[48,384]{1,0:T(8,128)(2,1)} %param.16) | copy-start | bytes 110596
  4.3 0.8 %copy-start.3 = (bf16[384,48]{0,1:T(8,128)(2,1)S(1)}, bf16[384,48]{0,1:T(8,128)(2,1)}, u32[]{:S(2)}) copy-start(bf16[384,48]{0,1:T(8,128)(2,1)} %param.14) | copy-start | bytes 110596
  4.4 0.9 %copy-start = (bf16[8,32,384]{2,1,0:T(8,128)(2,1)S(1)}, bf16[8,32,384]{2,1,0:T(8,128)(2,1)}, u32[]{:S(2)}) copy-start(bf16[8,32,384]{2,1,0:T(8,128)(2,1)} %x_ref.1) | copy-start | bytes 589828
  4.4 1.0 %copy-start.1 = (bf16[8,32,384]{2,1,0:T(8,128)(2,1)S(1)}, bf16[8,32,384]{2,1,0:T(8,128)(2,1)}, u32[]{:S(2)}) copy-start(bf16[8,32,384]{2,1,0:T(8,128)(2,1)} %cot_ref.1) | copy-start | bytes 589828

commit v2 on v1

--- a/solution.py
+++ b/solution.py
@@ -150,18 +150,29 @@
     rows,
     cols,
     orders,
-    x_ref,
-    taps_ref,
-    vec_ref,
-    bin_ref,
-    shard_ref,
-    cot_ref,
+    x_hbm,
+    taps_hbm,
+    gain_hbm,
+    offset_hbm,
+    win_hbm,
+    bin_hbm,
+    wout_hbm,
+    bout_hbm,
+    scale_hbm,
+    cot_hbm,
     out_ref,
     gin_ref,
     gwin_ref,
     gwout_ref,
     small_ref,
     gbin_ref,
+    cot_ref,
+    taps_ref,
+    gain_ref,
+    offset_ref,
+    bin_ref,
+    bout_ref,
+    scale_ref,
     xpad,
     gpad,
     wide,
@@ -176,7 +187,11 @@
     leaving,
     arriving,
     sums,
+    sums_first,
+    sums_run,
     sums_in,
+    sums_all,
+    local_sem,
     halo_send,
     halo_recv,
     gather_send,
@@ -186,11 +201,11 @@
     sum_send,
     sum_recv,
 ):
-    height, width, channels = x_ref.shape
+    height, width, channels = cot_ref.shape
     pixels = height * width
     parts = len(orders)
     steps = len(orders[0])
-    unit_rows = shard_ref.shape[2]
+    unit_rows = weights.shape[3]
     chunk = weights.shape[2] * unit_rows
     row, col = lax.axis_index("row"), lax.axis_index("col")
     me = row * cols + col
@@ -296,33 +311,90 @@
         if step:
             scatter_start(part, step - 1)
 
-    def scatter_turns(step):
-        for part in range(parts):
-            scatter_turn(part, step)
-
-    def sum_copy(step):
+    pair_bit = orders[0][-1]
+    pair_half = bit_of(pair_bit)
+    sum_orders = [orders[0][:-1], orders[0][:-1][::-1]]
+
+    def pair_copy():
         return pltpu.make_async_remote_copy(
-            src_ref=sums.at[step],
-            dst_ref=sums_in.at[step],
-            send_sem=sum_send.at[step],
-            recv_sem=sum_recv.at[step],
-            device_id=partner(orders[0][steps - 1 - step]),
+            src_ref=sums.at[pl.ds((1 - pair_half) * 2, 2)],
+            dst_ref=sums_first,
+            send_sem=sum_send.at[0],
+            recv_sem=sum_recv.at[0],
+            device_id=partner(pair_bit),
             device_id_type=MESH,
         )
 
+    def run_copy(step, half):
+        return pltpu.make_async_remote_copy(
+            src_ref=sums_run.at[step, half],
+            dst_ref=sums_in.at[step, half],
+            send_sem=sum_send.at[1 + 2 * step + half],
+            recv_sem=sum_recv.at[1 + 2 * step + half],
+            device_id=partner(sum_orders[half][step]),
+            device_id_type=MESH,
+        )
+
+    def share_copy():
+        own = sums_all.at[pl.ds(pair_half * 2, 2)]
+        return pltpu.make_async_remote_copy(
+            src_ref=own,
+            dst_ref=own,
+            send_sem=sum_send.at[2 * steps - 1],
+            recv_sem=sum_recv.at[2 * steps - 1],
+            device_id=partner(pair_bit),
+            device_id_type=MESH,
+        )
+
     def sum_turn(step):
-        sum_copy(step).wait()
-        sums[step + 1] = sums[step] + sums_in[step]
-        if step + 1 < steps:
-            sum_copy(step + 1).start()
-
-    gain, offset = vec_ref[0:1, :], vec_ref[1:2, :]
-    out_bias, scale = vec_ref[2:3, :], vec_ref[3:4, :]
-
+        last = steps - 1
+        if step == 0:
+            pair_copy().wait()
+            sums_run[0] = sums[pl.ds(pair_half * 2, 2)] + sums_first[...]
+        else:
+            for half in range(2):
+                run_copy(step - 1, half).wait()
+                added = sums_run[step - 1, half] + sums_in[step - 1, half]
+                if step < last:
+                    sums_run[step, half] = added
+                    run_copy(step, half).start()
+                else:
+                    sums_all[pl.ds(pair_half * 2 + half, 1)] = added[None]
+            if step == last:
+                share_copy().start()
+            return
+        for half in range(2):
+            run_copy(0, half).start()
+
+    def put_sum(at, lanes, value):
+        sums[at // 16, at % 16 : at % 16 + 1, lanes] = value
+
+    every = slice(0, channels)
     xpad[...] = jnp.zeros_like(xpad)
+    center = xpad.at[pl.ds(3, height), pl.ds(EDGE, width)]
+    moves = []
+    for part in range(parts):
+        for which, source in enumerate((win_hbm, wout_hbm)):
+            moves.append(
+                (source.at[pl.ds(part * unit_rows, unit_rows)], weights.at[part, which, places[part]])
+            )
+    moves += [
+        (x_hbm, center),
+        (cot_hbm, cot_ref),
+        (scale_hbm, scale_ref),
+        (taps_hbm, taps_ref),
+        (bin_hbm, bin_ref),
+        (gain_hbm, gain_ref),
+        (offset_hbm, offset_ref),
+        (bout_hbm, bout_ref),
+    ]
+    moves = [
+        pltpu.make_async_copy(source, target, local_sem.at[at])
+        for at, (source, target) in enumerate(moves)
+    ]
+    for move in moves:
+        move.start()
     gpad[...] = jnp.zeros_like(gpad)
-    for part in range(parts):
-        weights[part, :, pl.ds(places[part], 1)] = shard_ref[part][:, None]
 
     barrier = pltpu.get_barrier_semaphore()
     expected = steps
@@ -340,17 +412,41 @@
 
     pl.semaphore_wait(barrier, expected)
 
-    halo_start(x_ref, xpad, 0)
+    halo_start(x_hbm, xpad, 0)
+    for move in moves[: 2 * parts]:
+        move.wait()
     for part in range(parts):
         gather_turn(part, 0)
-
-    xpad[3 : 3 + height, EDGE : EDGE + width] = x_ref[...]
-    sums[0, 48:64] = jnp.zeros((16, channels), f32)
+    for move in moves[2 * parts :]:
+        move.wait()
+
+    def as_row(ref):
+        return ref[...].reshape(1, ref.shape[0])
+
+    gain, offset = as_row(gain_ref), as_row(offset_ref)
+    out_bias, scale = as_row(bout_ref), as_row(scale_ref)
+    sums[3] = jnp.zeros((16, channels), f32)
     grad_mixed = cot_ref[...].astype(f32).reshape(pixels, channels) * scale
     mixed_low[...] = grad_mixed.astype(bf16)
-    sums[0, 51:52] = jnp.sum(grad_mixed, 0, keepdims=True)
-
-    halo_wait(x_ref, xpad, 0)
+    put_sum(51, every, jnp.sum(grad_mixed, 0, keepdims=True))
+
+    owners = []
+    for order in orders:
+        owners.append(
+            [
+                sum(((place >> step) & 1) << b for step, b in enumerate(order))
+                for place in range(2**steps)
+            ]
+        )
+    bias_all = as_row(bin_ref)
+    biases = []
+    for part in range(parts):
+        starts = [(owner * parts + part) * unit_rows for owner in owners[part]]
+        biases.append(
+            jnp.concatenate([bias_all[:, at : at + unit_rows] for at in starts], 1)
+        )
+
+    halo_wait(x_hbm, xpad, 0)
     for part in range(parts):
         gather_turn(part, 1)
     wide[...] = xpad[:, 8 : width + 24].astype(f32)
@@ -363,9 +459,8 @@
         for tap_col in range(7):
             shifted = window(tap_col, lanes)
             for tap_row in range(7):
-                at = tap_row * 7 + tap_col
-                at = 48 - at if flip else at
-                result = result + shifted[tap_row : tap_row + height] * taps_ref[at : at + 1, lanes]
+                a, b = (6 - tap_row, 6 - tap_col) if flip else (tap_row, tap_col)
+                result = result + shifted[tap_row : tap_row + height] * taps_ref[a, b : b + 1, lanes]
         return result
 
     blocks = channels // LANES
@@ -381,16 +476,18 @@
     inv_std = lax.rsqrt(jnp.mean(centered * centered, -1, keepdims=True) + 1e-06)
     unit[...] = centered * inv_std
     normed[...] = (unit[...] * gain + offset).astype(bf16)
-    for step in range(blocks + 2, steps + 1):
+    for step in range(blocks + 2, steps):
         for part in range(parts):
             gather_turn(part, step)
 
+    bias_sums = []
     for part in range(parts):
+        gather_turn(part, steps)
         win = weights[part, 0].reshape(chunk, channels)
         wout = weights[part, 1].reshape(chunk, channels)
         hidden = (
             lax.dot_general(normed[...], win, CONTRACT_LAST, preferred_element_type=f32)
-            + bin_ref[part : part + 1, :]
+            + biases[part]
         )
         act_value, slope = gelu_parts(hidden)
         activated = act_value.astype(bf16)
@@ -409,18 +506,14 @@
         gnorm_term = jnp.dot(grad_hidden, win, preferred_element_type=f32)
         mixed[...] = mixed_term if part == 0 else mixed[...] + mixed_term
         gnorm[...] = gnorm_term if part == 0 else gnorm[...] + gnorm_term
-        bias_sum = jnp.sum(grad_hidden.astype(f32), 0, keepdims=True)
-        for piece in range(chunk // LANES):
-            at = part * (chunk // LANES) + piece
-            sums[0, 53 + at // blocks : 54 + at // blocks, at % blocks * LANES : (at % blocks + 1) * LANES] = (
-                bias_sum[:, piece * LANES : (piece + 1) * LANES]
-            )
-
-    scatter_turns(steps - 1)
+        bias_sums.append(jnp.sum(grad_hidden.astype(f32), 0, keepdims=True))
+        for earlier in range(part):
+            scatter_turn(earlier, steps - part + earlier)
+
     grad_normed = gnorm[...]
     unit_scaled = unit[...]
-    sums[0, 49:50] = jnp.sum(grad_normed * unit_scaled, 0, keepdims=True)
-    sums[0, 50:51] = jnp.sum(grad_normed, 0, keepdims=True)
+    put_sum(49, every, jnp.sum(grad_normed * unit_scaled, 0, keepdims=True))
+    put_sum(50, every, jnp.sum(grad_normed, 0, keepdims=True))
     scaled = grad_normed * gain
     grad_conv = inv_std * (
         scaled
@@ -432,12 +525,20 @@
     gpad[3 : 3 + height, EDGE : EDGE + width] = normed[...].reshape(height, width, channels)
     grad_block = gpad.at[pl.ds(3, height), pl.ds(EDGE, width)]
     halo_start(grad_block, gpad, 1)
+    scatter_turn(2, steps - 1)
 
     mixed_full = mixed[...] + out_bias
-    source = x_ref[...].astype(f32).reshape(pixels, channels)
+    source = center[...].astype(f32).reshape(pixels, channels)
     out_ref[...] = (source + scale * mixed_full).astype(bf16).reshape(height, width, channels)
     grad_flow = cot_ref[...].astype(f32).reshape(pixels, channels)
-    sums[0, 52:53] = jnp.sum(grad_flow * mixed_full, 0, keepdims=True)
+    put_sum(52, every, jnp.sum(grad_flow * mixed_full, 0, keepdims=True))
+    for line in range(4):
+        pieces = []
+        for owner in range(line * 2**steps // 4, (line + 1) * 2**steps // 4):
+            for part in range(parts):
+                at = owners[part].index(owner) * unit_rows
+                pieces.append(bias_sums[part][:, at : at + unit_rows])
+        put_sum(53 + line, every, jnp.concatenate(pieces, 1))
 
     for block in range(blocks):
         lanes = slice(block * LANES, (block + 1) * LANES)
@@ -447,13 +548,14 @@
             for tap_row in range(7):
                 at = tap_row * 7 + tap_col
                 term = shifted[tap_row : tap_row + height] * grad_part
-                sums[0, at : at + 1, lanes] = jnp.sum(
-                    term.reshape(pixels, LANES), 0, keepdims=True
-                )
+                put_sum(at, lanes, jnp.sum(term.reshape(pixels, LANES), 0, keepdims=True))
         if block == 0:
-            scatter_turns(steps - 2)
-    sum_copy(0).start()
-    scatter_turns(steps - 3)
+            scatter_turn(1, steps - 2)
+            scatter_turn(0, steps - 3)
+    pair_copy().start()
+    scatter_turn(2, steps - 2)
+    scatter_turn(1, steps - 3)
+    scatter_turn(0, steps - 4)
 
     halo_wait(grad_block, gpad, 1)
     wide[...] = gpad[:, 8 : width + 24].astype(f32)
@@ -463,19 +565,47 @@
             cot_ref[:, :, lanes].astype(f32) + stencil(lanes, True)
         ).astype(bf16)
         sum_turn(block)
-        if steps - 4 - block >= 0:
-            scatter_turns(steps - 4 - block)
-    for step in range(steps - 4 - blocks, -1, -1):
-        scatter_turns(step)
+        if block == 1:
+            scatter_turn(2, steps - 3)
+            scatter_turn(1, steps - 4)
+    pending = []
+    for part in range(parts):
+        for step in range(steps - 5 + max(part - 1, 0), -1, -1):
+            pending.append((part, step))
+    pending.sort(key=lambda turn: -turn[1])
     for step in range(blocks, steps):
+        for turn in pending[:2]:
+            scatter_turn(*turn)
+        pending = pending[2:]
         sum_turn(step)
+    for turn in pending:
+        scatter_turn(*turn)
+    share_copy().wait()
     for part in range(parts):
         at = slice(part * unit_rows, (part + 1) * unit_rows)
         own = total[part, :, pl.ds(places[part], 1)]
         gwin_ref[at, :] = own[0, 0]
         gwout_ref[at, :] = own[1, 0]
-    small_ref[...] = sums[steps, 0:53]
-    gbin_ref[...] = sums[steps, 53:57]
+    everything = sums_all[...].reshape(64, channels)
+    small_ref[...] = everything[0:53]
+    gbin_ref[...] = everything[53:57]
+
+
+def write_out(*refs):
+    count = (len(refs) - 2) // 2
+    sources, targets, line, sems = refs[:count], refs[count : 2 * count], refs[-2], refs[-1]
+    copies = []
+    for at in range(count):
+        source = sources[at]
+        if at == count - 1:
+            size = source.shape[1]
+            for row in range(source.shape[0]):
+                line[row * size : (row + 1) * size] = source[row]
+            source = line
+        copies.append(pltpu.make_async_copy(source, targets[at], sems.at[at]))
+        copies[-1].start()
+    for copy in copies:
+        copy.wait()
 
 
 def on_device(
@@ -504,15 +634,6 @@
     orders = bit_orders(rows, cols)
     piece = units // parts
     pixels = height * width
-    shard = jnp.stack([w_in.T, w_out]).reshape(2, parts, piece, channels).transpose(1, 0, 2, 3)
-    vectors = jnp.stack([ln_gain, ln_bias, b_out, layer_scale])
-    spread = b_in.reshape((2,) * steps + (parts, piece))
-    bias = jnp.stack(
-        [
-            spread[..., part, :].transpose([steps - 1 - b for b in order[::-1]] + [steps]).reshape(-1)
-            for part, order in enumerate(orders)
-        ]
-    )
     f32, bf16 = jnp.float32, jnp.bfloat16
     padded_shape = (height + 6, width + 2 * EDGE, channels)
     outs = pl.pallas_call(
@@ -525,9 +646,16 @@
             jax.ShapeDtypeStruct((53, channels), f32),
             jax.ShapeDtypeStruct((4, channels), f32),
         ),
-        in_specs=[pl.BlockSpec(memory_space=pltpu.VMEM)] * 6,
+        in_specs=[pl.BlockSpec(memory_space=pl.ANY)] * 10,
         out_specs=(pl.BlockSpec(memory_space=pltpu.VMEM),) * 6,
         scratch_shapes=[
+            pltpu.VMEM(cotangent.shape, bf16),
+            pltpu.VMEM(kernel.shape, f32),
+            pltpu.VMEM((channels,), f32),
+            pltpu.VMEM((channels,), f32),
+            pltpu.VMEM(b_in.shape, f32),
+            pltpu.VMEM((channels,), f32),
+            pltpu.VMEM((channels,), f32),
             pltpu.VMEM(padded_shape, bf16),
             pltpu.VMEM(padded_shape, bf16),
             pltpu.VMEM((height + 6, width + 16, channels), f32),
@@ -541,29 +669,47 @@
             pltpu.VMEM((parts, 2, devices, piece, channels), f32),
             pltpu.VMEM((parts, 2, devices, piece, channels), bf16),
             pltpu.VMEM((parts, 2, devices, piece, channels), bf16),
-            pltpu.VMEM((steps + 1, 64, channels), f32),
-            pltpu.VMEM((steps, 64, channels), f32),
+            pltpu.VMEM((4, 16, channels), f32),
+            pltpu.VMEM((2, 16, channels), f32),
+            pltpu.VMEM((steps - 1, 2, 16, channels), f32),
+            pltpu.VMEM((steps - 1, 2, 16, channels), f32),
+            pltpu.VMEM((4, 16, channels), f32),
+            pltpu.SemaphoreType.DMA((2 * parts + 8,)),
             pltpu.SemaphoreType.DMA((2, len(SIDES))),
             pltpu.SemaphoreType.DMA((2, len(SIDES))),
             pltpu.SemaphoreType.DMA((parts, steps)),
             pltpu.SemaphoreType.DMA((parts, steps)),
             pltpu.SemaphoreType.DMA((parts, steps)),
             pltpu.SemaphoreType.DMA((parts, steps)),
-            pltpu.SemaphoreType.DMA((steps,)),
-            pltpu.SemaphoreType.DMA((steps,)),
+            pltpu.SemaphoreType.DMA((2 * steps,)),
+            pltpu.SemaphoreType.DMA((2 * steps,)),
         ],
         compiler_params=pltpu.CompilerParams(
             collective_id=0, has_side_effects=True, vmem_limit_bytes=50 * 2**20
         ),
         name="convnext_block",
-    )(feature_map, kernel.reshape(49, channels), vectors, bias, shard, cotangent)
-    block_out, grad_input, grad_win, grad_wout, small_grads, bias_sums = outs
-    pieces = bias_sums.reshape((parts,) + (2,) * steps + (piece,))
-    ordered = []
-    for part, order in enumerate(orders):
-        back = [steps - 1 - order.index(b) for b in range(steps - 1, -1, -1)]
-        ordered.append(pieces[part].transpose(back + [steps]).reshape(devices, piece))
-    grad_b_in = jnp.stack(ordered, 1).reshape(-1)
+    )(
+        feature_map,
+        kernel,
+        ln_gain,
+        ln_bias,
+        w_in.T,
+        b_in,
+        w_out,
+        b_out,
+        layer_scale,
+        cotangent,
+    )
+    outs = pl.pallas_call(
+        write_out,
+        out_shape=tuple(jax.ShapeDtypeStruct(out.shape, out.dtype) for out in outs[:-1])
+        + (jax.ShapeDtypeStruct(b_in.shape, f32),),
+        in_specs=[pl.BlockSpec(memory_space=pltpu.VMEM)] * 6,
+        out_specs=(pl.BlockSpec(memory_space=pl.ANY),) * 6,
+        scratch_shapes=[pltpu.VMEM(b_in.shape, f32), pltpu.SemaphoreType.DMA((6,))],
+        name="write_out",
+    )(*outs)
+    block_out, grad_input, grad_win, grad_wout, small_grads, grad_b_in = outs
     return (block_out, grad_input, grad_win.T, grad_wout, small_grads, grad_b_in)
 
 

time: 75.5 us -> 83.3 us (1.10)
  Pallas kernels: 65.6 us -> 70.5 us
  local copies, waits for them, and re-layouts: 8.81 us -> 11.5 us
    unnamed x26 -> x32, local copies, waits for them, and re-layouts: 6.6 us -> 11.5 us
    pallas_call x1, Pallas kernels: 65.6 us -> 68.5 us  [on_device(): pl.pallas_call(functools.partial(fused_kernel, rows, cols, orders), out_s...]
    pallas_call x0 -> x1, Pallas kernels: none -> 2.02 us  [on_device(): pl.pallas_call(write_out, out_shape=tuple((jax.ShapeDtypeStruct(out.shape...]
    reshape x4 -> x0, local copies, waits for them, and re-layouts: 1.82 us -> none  [the longest x1 0.91 us: on_device(): kernel.reshape(49, channels)]
where the time goes in v2:
time: 83.3 us; the launch traced here: 82.8 us
  Pallas kernels  70.5 us (85%)
  local copies, waits for them, and re-layouts  11.5 us (14%)
  between operations  0.84 us (1%)
    pallas_call x1, Pallas kernels, on_device(): pl.pallas_call(functools.partial(fused_kernel, rows, cols, orders), out_s...  68.5 us
    unnamed x32, local copies, waits for them, and re-layouts  11.5 us
    pallas_call x1, Pallas kernels, on_device(): pl.pallas_call(write_out, out_shape=tuple((jax.ShapeDtypeStruct(out.shape...  2.02 us

profile of v2, /device:TPU:0, one launch (start us, length us, event | category | flops | bytes accessed | tf_op | source)
XLA Modules:
  0.0 82.8 jit_solution(5771544355054657054)
XLA Ops:
  0.6 0.0 copy-start.2
  0.6 0.9 %copy-done.2 = bf16[8,32,384]{2,1,0:T(8,128)(2,1)S(1)} copy-done((bf16[8,32,384]{2,1,0:T(8,128)(2,1)S(1)}, bf16[8,32,384]{2,1,0:T(8,128)(2,1)}, u32[]{:S(2)}) %copy-start.2) | copy-done | bytes 196632
  1.6 0.0 copy-start.3
  1.6 0.9 %copy-done.3 = bf16[8,32,384]{2,1,0:T(8,128)(2,1)S(1)} copy-done((bf16[8,32,384]{2,1,0:T(8,128)(2,1)S(1)}, bf16[8,32,384]{2,1,0:T(8,128)(2,1)}, u32[]{:S(2)}) %copy-start.3) | copy-done | bytes 196632
  2.5 0.0 copy-start.4
  2.5 0.9 %copy-done.4 = f32[7,7,384]{2,1,0:T(8,128)S(1)} copy-done((f32[7,7,384]{2,1,0:T(8,128)S(1)}, f32[7,7,384]{2,1,0:T(8,128)}, u32[]{:S(2)}) %copy-start.4) | copy-done | bytes 75288
  3.4 0.0 copy-start.8
  3.4 0.8 copy-done.8
  4.1 0.0 copy-start.9
  4.2 0.8 copy-done.9
  4.9 0.0 copy-start.10
  4.9 0.7 copy-done.10
  5.6 0.0 copy-start.12
  5.6 0.7 copy-done.12
  6.3 0.0 copy-start.13
  6.3 0.7 copy-done.13
  7.0 0.0 copy-start.14
  7.0 0.7 copy-done.14
  7.7 0.0 copy-start.15
  7.7 0.7 copy-done.15
  8.3 68.5 %convnext_block.1 = (bf16[8,32,384]{2,1,0:T(8,128)(2,1)S(1)}, bf16[8,32,384]{2,1,0:T(8,128)(2,1)S(1)}, f32[48,384]{1,0:T(8,128)S(1)}, f32[48,384]{1,0:T(8,128)S(...) custom-call(bf16[8,32,384]{2,1,0:T(8,128)(2,1)S(1)} %copy-done.2, f32[7,7,384]{2,1,0:T(8,128)S(1)} %copy-done.4, ...), custom_call_target="tpu_custom_call" | custom-call | tf_op jit(solution)/shard_map/convnext_block/pallas_call | solution.py:639
  76.8 0.0 copy-start
  76.8 0.7 copy-done
  77.5 0.0 copy-start.1
  77.5 0.7 copy-done.1
  78.2 0.0 copy-start.5
  78.2 0.6 copy-done.5
  78.8 0.0 copy-start.6
  78.8 0.6 copy-done.6
  79.4 0.0 copy-start.7
  79.4 0.6 copy-done.7
  80.1 0.0 copy-start.11
  80.1 0.6 copy-done.11
  80.7 2.0 %write_out.1 = (bf16[8,32,384]{2,1,0:T(8,128)(2,1)}, bf16[8,32,384]{2,1,0:T(8,128)(2,1)}, f32[48,384]{1,0:T(8,128)}, f32[48,384]{1,0:T(8,128)}, f32[53,384]{1,0:T(8,128)}, /*index=5*/f32[1536]{0:T(1024)}) custom-call(bf16[8,32,384]{2,1,0:T(8,128)(2,1)} %copy-done, bf16[8,32,384]{2,1,0:T(8,128)(2,1)} %copy-done.1, f32[48,384]{1,0:T(8,128)} %copy-done.6, ...), custom_call_target="tpu_custom_call" | custom-call | tf_op jit(solution)/shard_map/write_out/pallas_call | solution.py:703
Async XLA Ops:
  0.6 0.9 %copy-start.2 = (bf16[8,32,384]{2,1,0:T(8,128)(2,1)S(1)}, bf16[8,32,384]{2,1,0:T(8,128)(2,1)}, u32[]{:S(2)}) copy-start(bf16[8,32,384]{2,1,0:T(8,128)(2,1)} %x_hbm.1) | copy-start | bytes 589828
  1.6 0.9 %copy-start.3 = (bf16[8,32,384]{2,1,0:T(8,128)(2,1)S(1)}, bf16[8,32,384]{2,1,0:T(8,128)(2,1)}, u32[]{:S(2)}) copy-start(bf16[8,32,384]{2,1,0:T(8,128)(2,1)} %cot_hbm.1) | copy-start | bytes 589828
  2.5 0.9 %copy-start.4 = (f32[7,7,384]{2,1,0:T(8,128)S(1)}, f32[7,7,384]{2,1,0:T(8,128)}, u32[]{:S(2)}) copy-start(f32[7,7,384]{2,1,0:T(8,128)} %taps_hbm.1) | copy-start | bytes 225796
  3.4 0.8 copy-start.8
  4.1 0.8 copy-start.9
  4.9 0.7 copy-start.10
  5.6 0.7 copy-start.12
  6.3 0.7 copy-start.13
  7.0 0.7 copy-start.14
  7.7 0.7 copy-start.15
  76.8 0.7 copy-start
  77.5 0.7 copy-start.1
  78.2 0.6 copy-start.5
  78.8 0.6 copy-start.6
  79.4 0.6 copy-start.7
  80.1 0.6 copy-start.11

commit v3 on v2

--- a/solution.py
+++ b/solution.py
@@ -133,6 +133,7 @@
 MESH = pl.DeviceIdType.MESH
 SIDES = [(a, b) for a in (-1, 0, 1) for b in (-1, 0, 1) if (a, b) != (0, 0)]
 EDGE = 16
+TILE = 32
 LANES = 128
 CONTRACT_LAST = (((1,), (1,)), ((), ()))
 CONTRACT_FIRST = (((0,), (0,)), ((), ()))
@@ -160,12 +161,23 @@
     bout_hbm,
     scale_hbm,
     cot_hbm,
+    out_hbm,
+    gin_hbm,
+    gwin_hbm,
+    gwout_hbm,
+    small_hbm,
+    gbin_hbm,
     out_ref,
     gin_ref,
     gwin_ref,
     gwout_ref,
     small_ref,
     gbin_ref,
+    hid,
+    gact,
+    act,
+    ghid,
+    inv,
     cot_ref,
     taps_ref,
     gain_ref,
@@ -366,6 +378,13 @@
         for half in range(2):
             run_copy(0, half).start()
 
+    given = []
+
+    def give(source, target):
+        at = 2 * parts + 8 + len(given)
+        given.append(pltpu.make_async_copy(source, target, local_sem.at[at]))
+        given[-1].start()
+
     def put_sum(at, lanes, value):
         sums[at // 16, at % 16 : at % 16 + 1, lanes] = value
 
@@ -471,11 +490,18 @@
             for part in range(parts):
                 gather_turn(part, block + 2)
 
-    centered = conv[...]
-    centered = centered - jnp.mean(centered, -1, keepdims=True)
-    inv_std = lax.rsqrt(jnp.mean(centered * centered, -1, keepdims=True) + 1e-06)
-    unit[...] = centered * inv_std
-    normed[...] = (unit[...] * gain + offset).astype(bf16)
+    def norm_tile(tile, carry):
+        at = pl.ds(pl.multiple_of(tile * TILE, TILE), TILE)
+        centered = conv[at, :]
+        centered = centered - jnp.mean(centered, -1, keepdims=True)
+        inv_std = lax.rsqrt(jnp.mean(centered * centered, -1, keepdims=True) + 1e-06)
+        unit_scaled = centered * inv_std
+        inv[at, :] = inv_std
+        unit[at, :] = unit_scaled
+        normed[at, :] = (unit_scaled * gain + offset).astype(bf16)
+        return carry
+
+    lax.fori_loop(0, pixels // TILE, norm_tile, 0)
     for step in range(blocks + 2, steps):
         for part in range(parts):
             gather_turn(part, step)
@@ -485,16 +511,24 @@
         gather_turn(part, steps)
         win = weights[part, 0].reshape(chunk, channels)
         wout = weights[part, 1].reshape(chunk, channels)
-        hidden = (
-            lax.dot_general(normed[...], win, CONTRACT_LAST, preferred_element_type=f32)
-            + biases[part]
-        )
-        act_value, slope = gelu_parts(hidden)
-        activated = act_value.astype(bf16)
-        grad_act = lax.dot_general(
+        hid[...] = lax.dot_general(normed[...], win, CONTRACT_LAST, preferred_element_type=f32)
+        gact[...] = lax.dot_general(
             mixed_low[...], wout, CONTRACT_LAST, preferred_element_type=f32
         )
-        grad_hidden = (grad_act * slope).astype(bf16)
+
+        def gelu_tile(tile, bias_sum):
+            at = pl.ds(pl.multiple_of(tile * 16, 16), 16)
+            act_value, slope = gelu_parts(hid[at, :] + biases[part])
+            act[at, :] = act_value.astype(bf16)
+            low = (gact[at, :] * slope).astype(bf16)
+            ghid[at, :] = low
+            return bias_sum + low.astype(f32)
+
+        bias_sum = lax.fori_loop(
+            0, pixels // 16, gelu_tile, jnp.zeros((16, chunk), f32)
+        )
+        bias_sums.append(jnp.sum(bias_sum, 0, keepdims=True))
+        activated, grad_hidden = act[...], ghid[...]
         total[part, 1] = lax.dot_general(
             activated, mixed_low[...], CONTRACT_FIRST, preferred_element_type=f32
         ).reshape(-1, unit_rows, channels)
@@ -506,22 +540,32 @@
         gnorm_term = jnp.dot(grad_hidden, win, preferred_element_type=f32)
         mixed[...] = mixed_term if part == 0 else mixed[...] + mixed_term
         gnorm[...] = gnorm_term if part == 0 else gnorm[...] + gnorm_term
-        bias_sums.append(jnp.sum(grad_hidden.astype(f32), 0, keepdims=True))
-        for earlier in range(part):
-            scatter_turn(earlier, steps - part + earlier)
-
-    grad_normed = gnorm[...]
-    unit_scaled = unit[...]
-    put_sum(49, every, jnp.sum(grad_normed * unit_scaled, 0, keepdims=True))
-    put_sum(50, every, jnp.sum(grad_normed, 0, keepdims=True))
-    scaled = grad_normed * gain
-    grad_conv = inv_std * (
-        scaled
-        - jnp.mean(scaled, -1, keepdims=True)
-        - unit_scaled * jnp.mean(scaled * unit_scaled, -1, keepdims=True)
-    )
-    conv[...] = grad_conv
-    normed[...] = grad_conv.astype(bf16)
+        if part:
+            scatter_turn(part - 1, steps - 1)
+
+    def back_tile(tile, carry):
+        gain_sum, offset_sum = carry
+        at = pl.ds(pl.multiple_of(tile * TILE, TILE), TILE)
+        grad_normed = gnorm[at, :]
+        unit_scaled = unit[at, :]
+        product = grad_normed * unit_scaled
+        scaled = grad_normed * gain
+        grad_conv = inv[at, :] * (
+            scaled
+            - jnp.mean(scaled, -1, keepdims=True)
+            - unit_scaled * jnp.mean(scaled * unit_scaled, -1, keepdims=True)
+        )
+        conv[at, :] = grad_conv
+        normed[at, :] = grad_conv.astype(bf16)
+        return (
+            gain_sum + jnp.sum(product, 0, keepdims=True),
+            offset_sum + jnp.sum(grad_normed, 0, keepdims=True),
+        )
+
+    none = jnp.zeros((1, channels), f32)
+    gain_sum, offset_sum = lax.fori_loop(0, pixels // TILE, back_tile, (none, none))
+    put_sum(49, every, gain_sum)
+    put_sum(50, every, offset_sum)
     gpad[3 : 3 + height, EDGE : EDGE + width] = normed[...].reshape(height, width, channels)
     grad_block = gpad.at[pl.ds(3, height), pl.ds(EDGE, width)]
     halo_start(grad_block, gpad, 1)
@@ -539,6 +583,7 @@
                 at = owners[part].index(owner) * unit_rows
                 pieces.append(bias_sums[part][:, at : at + unit_rows])
         put_sum(53 + line, every, jnp.concatenate(pieces, 1))
+    give(out_ref, out_hbm)
 
     for block in range(blocks):
         lanes = slice(block * LANES, (block + 1) * LANES)
@@ -550,12 +595,11 @@
                 term = shifted[tap_row : tap_row + height] * grad_part
                 put_sum(at, lanes, jnp.sum(term.reshape(pixels, LANES), 0, keepdims=True))
         if block == 0:
+            scatter_turn(0, steps - 2)
             scatter_turn(1, steps - 2)
-            scatter_turn(0, steps - 3)
     pair_copy().start()
-    scatter_turn(2, steps - 2)
-    scatter_turn(1, steps - 3)
-    scatter_turn(0, steps - 4)
+    for part in (2, 0, 1):
+        scatter_turn(part, steps - 2 if part == 2 else steps - 3)
 
     halo_wait(grad_block, gpad, 1)
     wide[...] = gpad[:, 8 : width + 24].astype(f32)
@@ -567,43 +611,43 @@
         sum_turn(block)
         if block == 1:
             scatter_turn(2, steps - 3)
-            scatter_turn(1, steps - 4)
-    pending = []
-    for part in range(parts):
-        for step in range(steps - 5 + max(part - 1, 0), -1, -1):
-            pending.append((part, step))
-    pending.sort(key=lambda turn: -turn[1])
+    give(gin_ref, gin_hbm)
+    turn = steps - 4
     for step in range(blocks, steps):
-        for turn in pending[:2]:
-            scatter_turn(*turn)
-        pending = pending[2:]
+        if turn >= 0:
+            for part in range(parts):
+                scatter_turn(part, turn)
+            turn -= 1
         sum_turn(step)
-    for turn in pending:
-        scatter_turn(*turn)
-    share_copy().wait()
+    for step in range(turn, -1, -1):
+        for part in range(parts):
+            scatter_turn(part, step)
     for part in range(parts):
         at = slice(part * unit_rows, (part + 1) * unit_rows)
         own = total[part, :, pl.ds(places[part], 1)]
         gwin_ref[at, :] = own[0, 0]
         gwout_ref[at, :] = own[1, 0]
+    give(gwin_ref, gwin_hbm)
+    give(gwout_ref, gwout_hbm)
+    share_copy().wait()
     everything = sums_all[...].reshape(64, channels)
     small_ref[...] = everything[0:53]
-    gbin_ref[...] = everything[53:57]
+    for line in range(4):
+        gbin_ref[line * channels : (line + 1) * channels] = everything[53 + line]
+    give(small_ref, small_hbm)
+    give(gbin_ref, gbin_hbm)
+    for move in given:
+        move.wait()
 
 
 def write_out(*refs):
-    count = (len(refs) - 2) // 2
-    sources, targets, line, sems = refs[:count], refs[count : 2 * count], refs[-2], refs[-1]
-    copies = []
-    for at in range(count):
-        source = sources[at]
-        if at == count - 1:
-            size = source.shape[1]
-            for row in range(source.shape[0]):
-                line[row * size : (row + 1) * size] = source[row]
-            source = line
-        copies.append(pltpu.make_async_copy(source, targets[at], sems.at[at]))
-        copies[-1].start()
+    count = len(refs) // 2
+    sems = refs[-1]
+    copies = [
+        pltpu.make_async_copy(refs[at], refs[count + at], sems.at[at]) for at in range(count)
+    ]
+    for copy in copies:
+        copy.start()
     for copy in copies:
         copy.wait()
 
@@ -644,11 +688,22 @@
             jax.ShapeDtypeStruct((units, channels), f32),
             jax.ShapeDtypeStruct((units, channels), f32),
             jax.ShapeDtypeStruct((53, channels), f32),
-            jax.ShapeDtypeStruct((4, channels), f32),
+            jax.ShapeDtypeStruct(b_in.shape, f32),
         ),
-        in_specs=[pl.BlockSpec(memory_space=pl.ANY)] * 10,
-        out_specs=(pl.BlockSpec(memory_space=pltpu.VMEM),) * 6,
+        in_specs=[pl.BlockSpec(memory_space=pltpu.HBM)] * 10,
+        out_specs=(pl.BlockSpec(memory_space=pltpu.HBM),) * 6,
         scratch_shapes=[
+            pltpu.VMEM(cotangent.shape, bf16),
+            pltpu.VMEM(cotangent.shape, bf16),
+            pltpu.VMEM((units, channels), f32),
+            pltpu.VMEM((units, channels), f32),
+            pltpu.VMEM((53, channels), f32),
+            pltpu.VMEM(b_in.shape, f32),
+            pltpu.VMEM((pixels, devices * piece), f32),
+            pltpu.VMEM((pixels, devices * piece), f32),
+            pltpu.VMEM((pixels, devices * piece), bf16),
+            pltpu.VMEM((pixels, devices * piece), bf16),
+            pltpu.VMEM((pixels, 1), f32),
             pltpu.VMEM(cotangent.shape, bf16),
             pltpu.VMEM(kernel.shape, f32),
             pltpu.VMEM((channels,), f32),
@@ -674,7 +729,7 @@
             pltpu.VMEM((steps - 1, 2, 16, channels), f32),
             pltpu.VMEM((steps - 1, 2, 16, channels), f32),
             pltpu.VMEM((4, 16, channels), f32),
-            pltpu.SemaphoreType.DMA((2 * parts + 8,)),
+            pltpu.SemaphoreType.DMA((2 * parts + 14,)),
             pltpu.SemaphoreType.DMA((2, len(SIDES))),
             pltpu.SemaphoreType.DMA((2, len(SIDES))),
             pltpu.SemaphoreType.DMA((parts, steps)),
@@ -685,7 +740,7 @@
             pltpu.SemaphoreType.DMA((2 * steps,)),
         ],
         compiler_params=pltpu.CompilerParams(
-            collective_id=0, has_side_effects=True, vmem_limit_bytes=50 * 2**20
+            collective_id=0, has_side_effects=True, vmem_limit_bytes=60 * 2**20
         ),
         name="convnext_block",
     )(
@@ -702,11 +757,11 @@
     )
     outs = pl.pallas_call(
         write_out,
-        out_shape=tuple(jax.ShapeDtypeStruct(out.shape, out.dtype) for out in outs[:-1])
-        + (jax.ShapeDtypeStruct(b_in.shape, f32),),
-        in_specs=[pl.BlockSpec(memory_space=pltpu.VMEM)] * 6,
-        out_specs=(pl.BlockSpec(memory_space=pl.ANY),) * 6,
-        scratch_shapes=[pltpu.VMEM(b_in.shape, f32), pltpu.SemaphoreType.DMA((6,))],
+        out_shape=tuple(jax.ShapeDtypeStruct(out.shape, out.dtype) for out in outs),
+        in_specs=[pl.BlockSpec(memory_space=pltpu.HBM)] * 6,
+        out_specs=(pl.BlockSpec(memory_space=pltpu.HBM),) * 6,
+        scratch_shapes=[pltpu.SemaphoreType.DMA((6,))],
+        compiler_params=pltpu.CompilerParams(vmem_limit_bytes=60 * 2**20),
         name="write_out",
     )(*outs)
     block_out, grad_input, grad_win, grad_wout, small_grads, grad_b_in = outs

time: 83.3 us -> 85.2 us (1.023)
  Pallas kernels: 70.5 us -> 84.2 us
  local copies, waits for them, and re-layouts: 11.5 us -> 0 us
    pallas_call x1, Pallas kernels: 2.02 us -> 20.3 us  [on_device(): pl.pallas_call(write_out, out_shape=tuple((jax.ShapeDtypeStruct(out.shape...]
    unnamed x32 -> x0, local copies, waits for them, and re-layouts: 11.5 us -> none
    pallas_call x1, Pallas kernels: 68.5 us -> 63.9 us  [on_device(): pl.pallas_call(functools.partial(fused_kernel, rows, cols, orders), out_s...]
where the time goes in v3:
time: 85.2 us; the launch traced here: 85 us
  Pallas kernels  84.2 us (99%)
    pallas_call x1, Pallas kernels, on_device(): pl.pallas_call(functools.partial(fused_kernel, rows, cols, orders), out_s...  63.9 us
    pallas_call x1, Pallas kernels, on_device(): pl.pallas_call(write_out, out_shape=tuple((jax.ShapeDtypeStruct(out.shape...  20.3 us

profile of v3, /device:TPU:0, one launch (start us, length us, event | category | flops | bytes accessed | tf_op | source)
XLA Modules:
  0.0 85.0 jit_solution(2277754934560558688)
XLA Ops:
  0.6 63.9 %convnext_block.1 = (bf16[8,32,384]{2,1,0:T(8,128)(2,1)}, bf16[8,32,384]{2,1,0:T(8,128)(2,1)}, f32[48,384]{1,0:T(8,128)}, f32[48,384]{1,0:T(8,128)}, f32[53,384]{1,0:T(8,128)}, /*index=5*/f32[1536]{0:T(1024)}) custom-call(bf16[8,32,384]{2,1,0:T(8,128)(2,1)} %x_hbm.1, f32[7,7,384]{2,1,0:T(8,128)} %taps_hbm.1, f32[384]{0:T(512)} %gain_hbm.1, f32[384]{0:T(512)} %offset_hbm.1, ...), custom_call_target="tpu_custom_call" | custom-call | tf_op jit(solution)/shard_map/convnext_block/pallas_call | solution.py:683
  64.5 20.3 %write_out.1 = (bf16[8,32,384]{2,1,0:T(8,128)(2,1)}, bf16[8,32,384]{2,1,0:T(8,128)(2,1)}, f32[48,384]{1,0:T(8,128)}, f32[48,384]{1,0:T(8,128)}, f32[53,384]{1,0:T(8,128)}, /*index=5*/f32[1536]{0:T(1024)}) custom-call(bf16[8,32,384]{2,1,0:T(8,128)(2,1)} %get-tuple-element.18.refs_0_, bf16[8,32,384]{2,1,0:T(8,128)(2,1)} %get-tuple-element.19.refs_1_, ...), custom_call_target="tpu_custom_call" | custom-call | tf_op jit(solution)/shard_map/write_out/pallas_call | solution.py:758

commit v4 on v3

--- a/solution.py
+++ b/solution.py
@@ -161,12 +161,6 @@
     bout_hbm,
     scale_hbm,
     cot_hbm,
-    out_hbm,
-    gin_hbm,
-    gwin_hbm,
-    gwout_hbm,
-    small_hbm,
-    gbin_hbm,
     out_ref,
     gin_ref,
     gwin_ref,
@@ -378,13 +372,6 @@
         for half in range(2):
             run_copy(0, half).start()
 
-    given = []
-
-    def give(source, target):
-        at = 2 * parts + 8 + len(given)
-        given.append(pltpu.make_async_copy(source, target, local_sem.at[at]))
-        given[-1].start()
-
     def put_sum(at, lanes, value):
         sums[at // 16, at % 16 : at % 16 + 1, lanes] = value
 
@@ -449,6 +436,9 @@
     mixed_low[...] = grad_mixed.astype(bf16)
     put_sum(51, every, jnp.sum(grad_mixed, 0, keepdims=True))
 
+    for part in range(parts):
+        gather_turn(part, 1)
+
     owners = []
     for order in orders:
         owners.append(
@@ -466,8 +456,6 @@
         )
 
     halo_wait(x_hbm, xpad, 0)
-    for part in range(parts):
-        gather_turn(part, 1)
     wide[...] = xpad[:, 8 : width + 24].astype(f32)
 
     def window(shift, lanes):
@@ -486,9 +474,9 @@
     for block in range(blocks):
         lanes = slice(block * LANES, (block + 1) * LANES)
         conv[:, lanes] = stencil(lanes, False).reshape(pixels, LANES)
-        if block + 2 < steps:
+        if block == 0:
             for part in range(parts):
-                gather_turn(part, block + 2)
+                gather_turn(part, 2)
 
     def norm_tile(tile, carry):
         at = pl.ds(pl.multiple_of(tile * TILE, TILE), TILE)
@@ -502,7 +490,7 @@
         return carry
 
     lax.fori_loop(0, pixels // TILE, norm_tile, 0)
-    for step in range(blocks + 2, steps):
+    for step in range(3, steps):
         for part in range(parts):
             gather_turn(part, step)
 
@@ -583,7 +571,6 @@
                 at = owners[part].index(owner) * unit_rows
                 pieces.append(bias_sums[part][:, at : at + unit_rows])
         put_sum(53 + line, every, jnp.concatenate(pieces, 1))
-    give(out_ref, out_hbm)
 
     for block in range(blocks):
         lanes = slice(block * LANES, (block + 1) * LANES)
@@ -594,12 +581,11 @@
                 at = tap_row * 7 + tap_col
                 term = shifted[tap_row : tap_row + height] * grad_part
                 put_sum(at, lanes, jnp.sum(term.reshape(pixels, LANES), 0, keepdims=True))
-        if block == 0:
-            scatter_turn(0, steps - 2)
-            scatter_turn(1, steps - 2)
+        if block < 2:
+            scatter_turn(block, steps - 2)
     pair_copy().start()
-    for part in (2, 0, 1):
-        scatter_turn(part, steps - 2 if part == 2 else steps - 3)
+    scatter_turn(2, steps - 2)
+    scatter_turn(0, steps - 3)
 
     halo_wait(grad_block, gpad, 1)
     wide[...] = gpad[:, 8 : width + 24].astype(f32)
@@ -609,35 +595,28 @@
             cot_ref[:, :, lanes].astype(f32) + stencil(lanes, True)
         ).astype(bf16)
         sum_turn(block)
-        if block == 1:
+        if block == 0:
+            scatter_turn(1, steps - 3)
+        elif block == 2:
             scatter_turn(2, steps - 3)
-    give(gin_ref, gin_hbm)
-    turn = steps - 4
+    pending = [(part, step) for step in range(steps - 4, -1, -1) for part in range(parts)]
     for step in range(blocks, steps):
-        if turn >= 0:
-            for part in range(parts):
-                scatter_turn(part, turn)
-            turn -= 1
+        for turn in pending[:2]:
+            scatter_turn(*turn)
+        pending = pending[2:]
         sum_turn(step)
-    for step in range(turn, -1, -1):
-        for part in range(parts):
-            scatter_turn(part, step)
+    for turn in pending:
+        scatter_turn(*turn)
     for part in range(parts):
         at = slice(part * unit_rows, (part + 1) * unit_rows)
         own = total[part, :, pl.ds(places[part], 1)]
         gwin_ref[at, :] = own[0, 0]
         gwout_ref[at, :] = own[1, 0]
-    give(gwin_ref, gwin_hbm)
-    give(gwout_ref, gwout_hbm)
     share_copy().wait()
     everything = sums_all[...].reshape(64, channels)
     small_ref[...] = everything[0:53]
     for line in range(4):
         gbin_ref[line * channels : (line + 1) * channels] = everything[53 + line]
-    give(small_ref, small_hbm)
-    give(gbin_ref, gbin_hbm)
-    for move in given:
-        move.wait()
 
 
 def write_out(*refs):
@@ -691,14 +670,8 @@
             jax.ShapeDtypeStruct(b_in.shape, f32),
         ),
         in_specs=[pl.BlockSpec(memory_space=pltpu.HBM)] * 10,
-        out_specs=(pl.BlockSpec(memory_space=pltpu.HBM),) * 6,
+        out_specs=(pl.BlockSpec(memory_space=pltpu.VMEM),) * 6,
         scratch_shapes=[
-            pltpu.VMEM(cotangent.shape, bf16),
-            pltpu.VMEM(cotangent.shape, bf16),
-            pltpu.VMEM((units, channels), f32),
-            pltpu.VMEM((units, channels), f32),
-            pltpu.VMEM((53, channels), f32),
-            pltpu.VMEM(b_in.shape, f32),
             pltpu.VMEM((pixels, devices * piece), f32),
             pltpu.VMEM((pixels, devices * piece), f32),
             pltpu.VMEM((pixels, devices * piece), bf16),
@@ -729,7 +702,7 @@
             pltpu.VMEM((steps - 1, 2, 16, channels), f32),
             pltpu.VMEM((steps - 1, 2, 16, channels), f32),
             pltpu.VMEM((4, 16, channels), f32),
-            pltpu.SemaphoreType.DMA((2 * parts + 14,)),
+            pltpu.SemaphoreType.DMA((2 * parts + 8,)),
             pltpu.SemaphoreType.DMA((2, len(SIDES))),
             pltpu.SemaphoreType.DMA((2, len(SIDES))),
             pltpu.SemaphoreType.DMA((parts, steps)),
@@ -740,7 +713,7 @@
             pltpu.SemaphoreType.DMA((2 * steps,)),
         ],
         compiler_params=pltpu.CompilerParams(
-            collective_id=0, has_side_effects=True, vmem_limit_bytes=60 * 2**20
+            collective_id=0, has_side_effects=True, vmem_limit_bytes=32 * 2**20
         ),
         name="convnext_block",
     )(
@@ -758,10 +731,10 @@
     outs = pl.pallas_call(
         write_out,
         out_shape=tuple(jax.ShapeDtypeStruct(out.shape, out.dtype) for out in outs),
-        in_specs=[pl.BlockSpec(memory_space=pltpu.HBM)] * 6,
+        in_specs=[pl.BlockSpec(memory_space=pltpu.VMEM)] * 6,
         out_specs=(pl.BlockSpec(memory_space=pltpu.HBM),) * 6,
         scratch_shapes=[pltpu.SemaphoreType.DMA((6,))],
-        compiler_params=pltpu.CompilerParams(vmem_limit_bytes=60 * 2**20),
+        compiler_params=pltpu.CompilerParams(vmem_limit_bytes=4 * 2**20),
         name="write_out",
     )(*outs)
     block_out, grad_input, grad_win, grad_wout, small_grads, grad_b_in = outs

time: 85.2 us -> 70.4 us (0.83)
  Pallas kernels: 84.2 us -> 61.4 us
  local copies, waits for them, and re-layouts: 0 us -> 7.69 us
    pallas_call x1, Pallas kernels: 20.3 us -> 0.87 us  [on_device(): pl.pallas_call(write_out, out_shape=tuple((jax.ShapeDtypeStruct(out.shape...]
    unnamed x0 -> x20, local copies, waits for them, and re-layouts: none -> 7.69 us
    pallas_call x1, Pallas kernels: 63.9 us -> 60.5 us  [on_device(): pl.pallas_call(functools.partial(fused_kernel, rows, cols, orders), out_s...]
where the time goes in v4:
time: 70.4 us; the launch traced here: 69.9 us
  Pallas kernels  61.4 us (87%)
  local copies, waits for them, and re-layouts  7.69 us (11%)
  between operations  0.82 us (1%)
    pallas_call x1, Pallas kernels, on_device(): pl.pallas_call(functools.partial(fused_kernel, rows, cols, orders), out_s...  60.5 us
    unnamed x20, local copies, waits for them, and re-layouts  7.69 us

profile of v4, /device:TPU:0, one launch (start us, length us, event | category | flops | bytes accessed | tf_op | source)
XLA Modules:
  0.0 69.9 jit_solution(2673275636828084940)
XLA Ops:
  0.6 0.0 copy-start
  0.6 0.9 %copy-done = bf16[8,32,384]{2,1,0:T(8,128)(2,1)S(1)} copy-done((bf16[8,32,384]{2,1,0:T(8,128)(2,1)S(1)}, bf16[8,32,384]{2,1,0:T(8,128)(2,1)}, u32[]{:S(2)}) %copy-start) | copy-done | bytes 196632
  1.6 0.0 copy-start.1
  1.6 0.9 %copy-done.1 = bf16[8,32,384]{2,1,0:T(8,128)(2,1)S(1)} copy-done((bf16[8,32,384]{2,1,0:T(8,128)(2,1)S(1)}, bf16[8,32,384]{2,1,0:T(8,128)(2,1)}, u32[]{:S(2)}) %copy-start.1) | copy-done | bytes 196632
  2.5 0.0 copy-start.2
  2.5 0.9 %copy-done.2 = f32[7,7,384]{2,1,0:T(8,128)S(1)} copy-done((f32[7,7,384]{2,1,0:T(8,128)S(1)}, f32[7,7,384]{2,1,0:T(8,128)}, u32[]{:S(2)}) %copy-start.2) | copy-done | bytes 75288
  3.4 0.0 copy-start.3
  3.4 0.8 %copy-done.3 = bf16[384,48]{0,1:T(8,128)(2,1)S(1)} copy-done((bf16[384,48]{0,1:T(8,128)(2,1)S(1)}, bf16[384,48]{0,1:T(8,128)(2,1)}, u32[]{:S(2)}) %copy-start.3) | copy-done | bytes 36888
  4.1 0.0 copy-start.4
  4.2 0.8 %copy-done.4 = bf16[48,384]{1,0:T(8,128)(2,1)S(1)} copy-done((bf16[48,384]{1,0:T(8,128)(2,1)S(1)}, bf16[48,384]{1,0:T(8,128)(2,1)}, u32[]{:S(2)}) %copy-start.4) | copy-done | bytes 36888
  4.9 0.0 copy-start.5
  4.9 0.7 copy-done.5
  5.6 0.0 copy-start.6
  5.6 0.7 copy-done.6
  6.3 0.0 copy-start.7
  6.3 0.7 copy-done.7
  7.0 0.0 copy-start.8
  7.0 0.7 copy-done.8
  7.7 0.0 copy-start.9
  7.7 0.7 copy-done.9
  8.3 60.5 %convnext_block.1 = (bf16[8,32,384]{2,1,0:T(8,128)(2,1)S(1)}, bf16[8,32,384]{2,1,0:T(8,128)(2,1)S(1)}, f32[48,384]{1,0:T(8,128)S(1)}, f32[48,384]{1,0:T(8,128)S(...) custom-call(bf16[8,32,384]{2,1,0:T(8,128)(2,1)S(1)} %copy-done, f32[7,7,384]{2,1,0:T(8,128)S(1)} %copy-done.2, ...), custom_call_target="tpu_custom_call" | custom-call | tf_op jit(solution)/shard_map/convnext_block/pallas_call | solution.py:662
  68.9 0.9 %write_out.1 = (bf16[8,32,384]{2,1,0:T(8,128)(2,1)}, bf16[8,32,384]{2,1,0:T(8,128)(2,1)}, f32[48,384]{1,0:T(8,128)}, f32[48,384]{1,0:T(8,128)}, f32[53,384]{1,0:T(8,128)}, /*index=5*/f32[1536]{0:T(1024)}) custom-call(bf16[8,32,384]{2,1,0:T(8,128)(2,1)S(1)} %get-tuple-element.18.refs_0_, bf16[8,32,384]{2,1,0:T(8,128)(2,1)S(1)} %get-tuple-element.19.refs_1_, ...), custom_call_target="tpu_custom_call" | custom-call | tf_op jit(solution)/shard_map/write_out/pallas_call | solution.py:731
Async XLA Ops:
  0.6 0.9 %copy-start = (bf16[8,32,384]{2,1,0:T(8,128)(2,1)S(1)}, bf16[8,32,384]{2,1,0:T(8,128)(2,1)}, u32[]{:S(2)}) copy-start(bf16[8,32,384]{2,1,0:T(8,128)(2,1)} %x_hbm.1) | copy-start | bytes 589828
  1.6 0.9 %copy-start.1 = (bf16[8,32,384]{2,1,0:T(8,128)(2,1)S(1)}, bf16[8,32,384]{2,1,0:T(8,128)(2,1)}, u32[]{:S(2)}) copy-start(bf16[8,32,384]{2,1,0:T(8,128)(2,1)} %cot_hbm.1) | copy-start | bytes 589828
  2.5 0.9 %copy-start.2 = (f32[7,7,384]{2,1,0:T(8,128)S(1)}, f32[7,7,384]{2,1,0:T(8,128)}, u32[]{:S(2)}) copy-start(f32[7,7,384]{2,1,0:T(8,128)} %taps_hbm.1) | copy-start | bytes 225796
  3.4 0.8 %copy-start.3 = (bf16[384,48]{0,1:T(8,128)(2,1)S(1)}, bf16[384,48]{0,1:T(8,128)(2,1)}, u32[]{:S(2)}) copy-start(bf16[384,48]{0,1:T(8,128)(2,1)} %param.14) | copy-start | bytes 110596
  4.1 0.8 %copy-start.4 = (bf16[48,384]{1,0:T(8,128)(2,1)S(1)}, bf16[48,384]{1,0:T(8,128)(2,1)}, u32[]{:S(2)}) copy-start(bf16[48,384]{1,0:T(8,128)(2,1)} %wout_hbm.1) | copy-start | bytes 110596
  4.9 0.7 copy-start.5
  5.6 0.7 copy-start.6
  6.3 0.7 copy-start.7
  7.0 0.7 copy-start.8
  7.7 0.7 copy-start.9

commit v5 on v4

--- a/solution.py
+++ b/solution.py
@@ -143,7 +143,7 @@
     bits = (rows * cols).bit_length() - 1
     pair = cols.bit_length() - 1
     rest = [b for b in range(bits - 1, -1, -1) if b != pair]
-    orders = [rest, rest[-1:] + rest[:-1], rest[-2:] + rest[:-2]]
+    orders = [rest[-2:] + rest[:-2], rest[-1:] + rest[:-1], rest]
     return [order + [pair] for order in orders]
 
 
@@ -713,7 +713,7 @@
             pltpu.SemaphoreType.DMA((2 * steps,)),
         ],
         compiler_params=pltpu.CompilerParams(
-            collective_id=0, has_side_effects=True, vmem_limit_bytes=32 * 2**20
+            collective_id=0, has_side_effects=True, vmem_limit_bytes=60 * 2**20
         ),
         name="convnext_block",
     )(
@@ -734,7 +734,7 @@
         in_specs=[pl.BlockSpec(memory_space=pltpu.VMEM)] * 6,
         out_specs=(pl.BlockSpec(memory_space=pltpu.HBM),) * 6,
         scratch_shapes=[pltpu.SemaphoreType.DMA((6,))],
-        compiler_params=pltpu.CompilerParams(vmem_limit_bytes=4 * 2**20),
+        compiler_params=pltpu.CompilerParams(vmem_limit_bytes=60 * 2**20),
         name="write_out",
     )(*outs)
     block_out, grad_input, grad_win, grad_wout, small_grads, grad_b_in = outs

time: 70.4 us -> 63 us (0.89)
  local copies, waits for them, and re-layouts: 7.69 us -> 0 us
    unnamed x20 -> x0, local copies, waits for them, and re-layouts: 7.69 us -> none
    pallas_call x1, Pallas kernels: 0.87 us -> 2.03 us  [on_device(): pl.pallas_call(write_out, out_shape=tuple((jax.ShapeDtypeStruct(out.shape...]
where the time goes in v5:
time: 63 us; the launch traced here: 62.8 us
  Pallas kernels  62 us (98%)
  between operations  0.8 us (1%)
    pallas_call x1, Pallas kernels, on_device(): pl.pallas_call(functools.partial(fused_kernel, rows, cols, orders), out_s...  60 us
    pallas_call x1, Pallas kernels, on_device(): pl.pallas_call(write_out, out_shape=tuple((jax.ShapeDtypeStruct(out.shape...  2.03 us

profile of v5, /device:TPU:0, one launch (start us, length us, event | category | flops | bytes accessed | tf_op | source)
XLA Modules:
  0.0 62.8 jit_solution(14801276147947517082)
XLA Ops:
  0.6 60.0 %convnext_block.1 = (bf16[8,32,384]{2,1,0:T(8,128)(2,1)}, bf16[8,32,384]{2,1,0:T(8,128)(2,1)}, f32[48,384]{1,0:T(8,128)}, f32[48,384]{1,0:T(8,128)}, f32[53,384]{1,0:T(8,128)}, /*index=5*/f32[1536]{0:T(1024)}) custom-call(bf16[8,32,384]{2,1,0:T(8,128)(2,1)} %x_hbm.1, f32[7,7,384]{2,1,0:T(8,128)} %taps_hbm.1, f32[384]{0:T(512)} %gain_hbm.1, f32[384]{0:T(512)} %offset_hbm.1, ...), custom_call_target="tpu_custom_call" | custom-call | tf_op jit(solution)/shard_map/convnext_block/pallas_call | solution.py:662
  60.7 2.0 %write_out.1 = (bf16[8,32,384]{2,1,0:T(8,128)(2,1)}, bf16[8,32,384]{2,1,0:T(8,128)(2,1)}, f32[48,384]{1,0:T(8,128)}, f32[48,384]{1,0:T(8,128)}, f32[53,384]{1,0:T(8,128)}, /*index=5*/f32[1536]{0:T(1024)}) custom-call(bf16[8,32,384]{2,1,0:T(8,128)(2,1)} %get-tuple-element.18.refs_0_, bf16[8,32,384]{2,1,0:T(8,128)(2,1)} %get-tuple-element.19.refs_1_, ...), custom_call_target="tpu_custom_call" | custom-call | tf_op jit(solution)/shard_map/write_out/pallas_call | solution.py:731
